TPU v7x, 32 devices: a whole 2x2x4 slice. The times are simulated.
32 devices in a mesh: dp: 4 (over y, core), fsdp: 8 (over z, x).
Axes of the slice: x: 2, y: 2, z: 4, core: 2. Of those that a mesh axis runs over, the one named last changes fastest.
Arguments:
- hidden: bfloat16 [256, 64, 768], P(('dp', 'fsdp')), may hold values from -6 to 6
- image_feats: bfloat16 [96, 257, 1408], P(('dp', 'fsdp')), may hold values from -12 to 12
- caption_counts: int32 [32, 3], P(('dp', 'fsdp')), may hold values from 1 to 5, 8 in all within a row
- text_lengths: int32 [256], P(('dp', 'fsdp')), may hold values from 1 to 32
- out_grad: bfloat16 [256, 64, 768], P(('dp', 'fsdp')), may hold values from -6 to 6
- self_query: bfloat16 [768, 768], P('fsdp'), may hold values from -0.21875 to 0.21875
- query_bias: bfloat16 [768], P('fsdp'), may hold values from -3 to 3
- self_key: bfloat16 [768, 768], P('fsdp'), may hold values from -0.21875 to 0.21875
- self_value: bfloat16 [768, 768], P('fsdp'), may hold values from -0.21875 to 0.21875
- value_bias: bfloat16 [768], P('fsdp'), may hold values from -3 to 3
- self_output: bfloat16 [768, 768], P('fsdp'), may hold values from -0.875 to 0.875
- output_bias: bfloat16 [768], P('fsdp'), may hold values from -3 to 3
- first_gain: bfloat16 [768], P('fsdp'), may hold values from 0.099609375 to 1.8984375
- first_shift: bfloat16 [768], P('fsdp'), may hold values from -3 to 3
- cross_query: bfloat16 [768, 768], P('fsdp'), may hold values from -0.21875 to 0.21875
- crossquery_bias: bfloat16 [768], P('fsdp'), may hold values from -3 to 3
- cross_key: bfloat16 [1408, 768], P('fsdp'), may hold values from -0.15625 to 0.15625
- cross_value: bfloat16 [1408, 768], P('fsdp'), may hold values from -0.15625 to 0.15625
- crossvalue_bias: bfloat16 [768], P('fsdp'), may hold values from -3 to 3
- cross_output: bfloat16 [768, 768], P('fsdp'), may hold values from -1.75 to 1.75
- crossoutput_bias: bfloat16 [768], P('fsdp'), may hold values from -3 to 3
- second_gain: bfloat16 [768], P('fsdp'), may hold values from 0.099609375 to 1.8984375
- second_shift: bfloat16 [768], P('fsdp'), may hold values from -3 to 3
- vision_gain: bfloat16 [1408], P('fsdp'), may hold values from 0.099609375 to 1.8984375
- vision_shift: bfloat16 [1408], P('fsdp'), may hold values from -3 to 3
- expand_weight: bfloat16 [768, 3072], P(None, 'fsdp'), may hold values from -0.21875 to 0.21875
- expand_bias: bfloat16 [3072], P('fsdp'), may hold values from -3 to 3
- contract_weight: bfloat16 [3072, 768], P('fsdp'), may hold values from -0.109375 to 0.109375
- contract_bias: bfloat16 [768], P('fsdp'), may hold values from -3 to 3
- third_gain: bfloat16 [768], P('fsdp'), may hold values from 0.099609375 to 1.8984375
- third_shift: bfloat16 [768], P('fsdp'), may hold values from -3 to 3
Outputs:
- layer_out: float32 [256, 64, 768], P(('dp', 'fsdp'))
- input_grad: float32 [256, 64, 768], P(('dp', 'fsdp'))
- self_query_grad: float32 [768, 768], P('fsdp')
- query_bias_grad: float32 [768], P('fsdp')
- self_key_grad: float32 [768, 768], P('fsdp')
- self_value_grad: float32 [768, 768], P('fsdp')
- value_bias_grad: float32 [768], P('fsdp')
- self_output_grad: float32 [768, 768], P('fsdp')
- output_bias_grad: float32 [768], P('fsdp')
- first_gain_grad: float32 [768], P('fsdp')
- first_shift_grad: float32 [768], P('fsdp')
- cross_query_grad: float32 [768, 768], P('fsdp')
- crossquery_bias_grad: float32 [768], P('fsdp')
- cross_key_grad: float32 [1408, 768], P('fsdp')
- cross_value_grad: float32 [1408, 768], P('fsdp')
- crossvalue_bias_grad: float32 [768], P('fsdp')
- cross_output_grad: float32 [768, 768], P('fsdp')
- crossoutput_bias_grad: float32 [768], P('fsdp')
- second_gain_grad: float32 [768], P('fsdp')
- second_shift_grad: float32 [768], P('fsdp')
- vision_gain_grad: float32 [1408], P('fsdp')
- vision_shift_grad: float32 [1408], P('fsdp')
- expand_weight_grad: float32 [768, 3072], P(None, 'fsdp')
- expand_bias_grad: float32 [3072], P('fsdp')
- contract_weight_grad: float32 [3072, 768], P('fsdp')
- contract_bias_grad: float32 [768], P('fsdp')
- third_gain_grad: float32 [768], P('fsdp')
- third_shift_grad: float32 [768], P('fsdp')
Inputs may be any that keep to these rules, and one draw needn't show every extreme that they name: `caption_counts`: each row sums to 8 and its largest entry is 5; images are shown by consecutive captions of their block in order.
All inputs are finite; a program needn't handle non-finite values.
Results may differ from a plain program's by a relative error of at most 0.025.
Values may be sent and summed in bfloat16 or wider, within the bound.
A program may use at most 192 MiB of HBM per device.

v0:
```python
import jax
import jax.numpy as jnp
from jax import lax
from jax.sharding import PartitionSpec as P

D = 768
HEADS = 12
HDIM = 64
PATCH = 257
NQ = 32
SEQ = 64


EPS = 1e-06


def norm_rows(values, gain_row, shift_row):
    center = values - jnp.mean(values, axis=-1, keepdims=True)
    spread = jnp.mean(center * center, axis=-1, keepdims=True)
    return center * lax.rsqrt(spread + EPS) * gain_row + shift_row


def softmax_rows(scores):
    row_top = jnp.max(scores, axis=-1, keepdims=True)
    shifted = jnp.exp(scores - row_top)
    return shifted / jnp.sum(shifted, axis=-1, keepdims=True)


def gelu_exact(values):
    return jax.nn.gelu(values, approximate=False)


def project(operand, weight):
    return jnp.einsum("...k,kn->...n", operand, weight, preferred_element_type=jnp.float32)


def project_back(upstream, weight):
    return jnp.einsum("...n,kn->...k", upstream, weight, preferred_element_type=jnp.float32)


def weight_grad(operand, upstream):
    flat_operand = operand.reshape(-1, operand.shape[-1])
    flat_upstream = upstream.reshape(-1, upstream.shape[-1])
    return lax.dot_general(
        flat_operand, flat_upstream, (((0,), (0,)), ((), ())), preferred_element_type=jnp.float32
    )


def bias_grad(upstream):
    return jnp.sum(upstream.reshape(-1, upstream.shape[-1]), axis=0, dtype=jnp.float32)


def heads_of(values):
    return values.reshape(values.shape[:-1] + (HEADS, HDIM))


def as_float(values):
    return values.astype(jnp.float32)


def local(
    hidden,
    image_feats,
    caption_counts,
    text_lengths,
    out_grad,
    self_query,
    query_bias,
    self_key,
    self_value,
    value_bias,
    self_output,
    output_bias,
    first_gain,
    first_shift,
    cross_query,
    crossquery_bias,
    cross_key,
    cross_value,
    crossvalue_bias,
    cross_output,
    crossoutput_bias,
    second_gain,
    second_shift,
    vision_gain,
    vision_shift,
    expand_weight,
    expand_bias,
    contract_weight,
    contract_bias,
    third_gain,
    third_shift,
):
    full = (
        lax.all_gather(self_query, "fsdp", axis=0, tiled=True),
        lax.all_gather(query_bias, "fsdp", axis=0, tiled=True),
        lax.all_gather(self_key, "fsdp", axis=0, tiled=True),
        lax.all_gather(self_value, "fsdp", axis=0, tiled=True),
        lax.all_gather(value_bias, "fsdp", axis=0, tiled=True),
        lax.all_gather(self_output, "fsdp", axis=0, tiled=True),
        lax.all_gather(output_bias, "fsdp", axis=0, tiled=True),
        lax.all_gather(first_gain, "fsdp", axis=0, tiled=True),
        lax.all_gather(first_shift, "fsdp", axis=0, tiled=True),
        lax.all_gather(cross_query, "fsdp", axis=0, tiled=True),
        lax.all_gather(crossquery_bias, "fsdp", axis=0, tiled=True),
        lax.all_gather(cross_key, "fsdp", axis=0, tiled=True),
        lax.all_gather(cross_value, "fsdp", axis=0, tiled=True),
        lax.all_gather(crossvalue_bias, "fsdp", axis=0, tiled=True),
        lax.all_gather(cross_output, "fsdp", axis=0, tiled=True),
        lax.all_gather(crossoutput_bias, "fsdp", axis=0, tiled=True),
        lax.all_gather(second_gain, "fsdp", axis=0, tiled=True),
        lax.all_gather(second_shift, "fsdp", axis=0, tiled=True),
        lax.all_gather(vision_gain, "fsdp", axis=0, tiled=True),
        lax.all_gather(vision_shift, "fsdp", axis=0, tiled=True),
        lax.all_gather(expand_weight, "fsdp", axis=1, tiled=True),
        lax.all_gather(expand_bias, "fsdp", axis=0, tiled=True),
        lax.all_gather(contract_weight, "fsdp", axis=0, tiled=True),
        lax.all_gather(contract_bias, "fsdp", axis=0, tiled=True),
        lax.all_gather(third_gain, "fsdp", axis=0, tiled=True),
        lax.all_gather(third_shift, "fsdp", axis=0, tiled=True),
    )
    (
        w_query,
        b_query,
        w_key,
        w_value,
        b_value,
        w_out,
        b_out,
        gain_one,
        shift_one,
        w_cquery,
        b_cquery,
        w_ckey,
        w_cvalue,
        b_cvalue,
        w_cout,
        b_cout,
        gain_two,
        shift_two,
        gain_vision,
        shift_vision,
        w_expand,
        b_expand,
        w_contract,
        b_contract,
        gain_three,
        shift_three,
    ) = full
    scaling = HDIM ** (-0.5)
    captions = hidden.shape[0]
    images = image_feats.shape[0]
    bounds = jnp.cumsum(caption_counts[0], dtype=jnp.int32)
    positions = jnp.arange(captions, dtype=jnp.int32)
    image_index = jnp.sum(
        (positions[:, None] >= bounds[None, :]).astype(jnp.int32), axis=1, dtype=jnp.int32
    )
    onehot = image_index[:, None] == jnp.arange(images, dtype=jnp.int32)[None, :]
    pick = onehot.astype(jnp.bfloat16)
    slots = jnp.arange(SEQ, dtype=jnp.int32)[None, :]
    key_valid = jnp.logical_or(slots < NQ, slots - NQ < text_lengths[:, None])
    query_low = (project(hidden, w_query) + as_float(b_query)).astype(jnp.bfloat16)
    key_low = project(hidden, w_key).astype(jnp.bfloat16)
    value_low = (project(hidden, w_value) + as_float(b_value)).astype(jnp.bfloat16)
    scores = (
        jnp.einsum(
            "cqhd,ckhd->chqk",
            heads_of(query_low),
            heads_of(key_low),
            preferred_element_type=jnp.float32,
        )
        * scaling
    )
    scores = jnp.where(key_valid[:, None, None, :], scores, -1000000000.0)
    probs, soft_back = jax.vjp(softmax_rows, scores)
    probs_low = probs.astype(jnp.bfloat16)
    mixed_low = (
        jnp.einsum(
            "chqk,ckhd->cqhd", probs_low, heads_of(value_low), preferred_element_type=jnp.float32
        )
        .reshape(captions, SEQ, D)
        .astype(jnp.bfloat16)
    )
    branch = project(mixed_low, w_out) + as_float(b_out)
    first, norm_back_one = jax.vjp(
        norm_rows, as_float(hidden) + branch, as_float(gain_one), as_float(shift_one)
    )
    query_rows = first[:, :NQ]
    cross_in = query_rows.astype(jnp.bfloat16)
    cquery_low = (project(cross_in, w_cquery) + as_float(b_cquery)).astype(jnp.bfloat16)
    expanded = jnp.einsum("ci,ipf->cpf", pick, image_feats, preferred_element_type=jnp.float32)
    vision_vals, vision_back = jax.vjp(
        norm_rows, expanded, as_float(gain_vision), as_float(shift_vision)
    )
    vision_low = vision_vals.astype(jnp.bfloat16)
    ckey_low = project(vision_low, w_ckey).astype(jnp.bfloat16)
    cvalue_low = (project(vision_low, w_cvalue) + as_float(b_cvalue)).astype(jnp.bfloat16)
    cscores = (
        jnp.einsum(
            "cqhd,ckhd->chqk",
            heads_of(cquery_low),
            heads_of(ckey_low),
            preferred_element_type=jnp.float32,
        )
        * scaling
    )
    cprobs, csoft_back = jax.vjp(softmax_rows, cscores)
    cprobs_low = cprobs.astype(jnp.bfloat16)
    cmixed_low = (
        jnp.einsum(
            "chqk,ckhd->cqhd", cprobs_low, heads_of(cvalue_low), preferred_element_type=jnp.float32
        )
        .reshape(captions, NQ, D)
        .astype(jnp.bfloat16)
    )
    cbranch = project(cmixed_low, w_cout) + as_float(b_cout)
    second, norm_back_two = jax.vjp(
        norm_rows, query_rows + cbranch, as_float(gain_two), as_float(shift_two)
    )
    joined = jnp.concatenate([second, first[:, NQ:]], axis=1)
    joined_low = joined.astype(jnp.bfloat16)
    widened = project(joined_low, w_expand) + as_float(b_expand)
    active, gelu_back = jax.vjp(gelu_exact, widened)
    active_low = active.astype(jnp.bfloat16)
    narrowed = project(active_low, w_contract) + as_float(b_contract)
    layer_out, norm_back_three = jax.vjp(
        norm_rows, joined + narrowed, as_float(gain_three), as_float(shift_three)
    )
    again = (
        lax.all_gather(self_query, "fsdp", axis=0, tiled=True),
        lax.all_gather(self_key, "fsdp", axis=0, tiled=True),
        lax.all_gather(self_value, "fsdp", axis=0, tiled=True),
        lax.all_gather(self_output, "fsdp", axis=0, tiled=True),
        lax.all_gather(cross_query, "fsdp", axis=0, tiled=True),
        lax.all_gather(cross_key, "fsdp", axis=0, tiled=True),
        lax.all_gather(cross_value, "fsdp", axis=0, tiled=True),
        lax.all_gather(cross_output, "fsdp", axis=0, tiled=True),
        lax.all_gather(expand_weight, "fsdp", axis=1, tiled=True),
        lax.all_gather(contract_weight, "fsdp", axis=0, tiled=True),
    )
    (
        back_query,
        back_key,
        back_value,
        back_out,
        back_cquery,
        back_ckey,
        back_cvalue,
        back_cout,
        back_expand,
        back_contract,
    ) = again
    grad_three_in, grad_gain_three, grad_shift_three = norm_back_three(as_float(out_grad))
    grad_narrow = grad_three_in.astype(jnp.bfloat16)
    grad_w_contract = weight_grad(active_low, grad_narrow)
    grad_b_contract = bias_grad(grad_narrow)
    (grad_wide,) = gelu_back(project_back(grad_narrow, back_contract))
    grad_wide_low = grad_wide.astype(jnp.bfloat16)
    grad_w_expand = weight_grad(joined_low, grad_wide_low)
    grad_b_expand = bias_grad(grad_wide_low)
    grad_joined = grad_three_in + project_back(grad_wide_low, back_expand)
    grad_two_in, grad_gain_two, grad_shift_two = norm_back_two(grad_joined[:, :NQ])
    grad_cbranch = grad_two_in.astype(jnp.bfloat16)
    grad_w_cout = weight_grad(cmixed_low, grad_cbranch)
    grad_b_cout = bias_grad(grad_cbranch)
    grad_cmixed = heads_of(project_back(grad_cbranch, back_cout).astype(jnp.bfloat16))
    grad_cprobs = jnp.einsum(
        "cqhd,ckhd->chqk", grad_cmixed, heads_of(cvalue_low), preferred_element_type=jnp.float32
    )
    grad_cvalue = (
        jnp.einsum("chqk,cqhd->ckhd", cprobs_low, grad_cmixed, preferred_element_type=jnp.float32)
        .reshape(captions, PATCH, D)
        .astype(jnp.bfloat16)
    )
    (grad_cscores,) = csoft_back(grad_cprobs)
    grad_cscores_low = grad_cscores.astype(jnp.bfloat16)
    grad_cquery = (
        (
            jnp.einsum(
                "chqk,ckhd->cqhd",
                grad_cscores_low,
                heads_of(ckey_low),
                preferred_element_type=jnp.float32,
            )
            * scaling
        )
        .reshape(captions, NQ, D)
        .astype(jnp.bfloat16)
    )
    grad_ckey = (
        (
            jnp.einsum(
                "chqk,cqhd->ckhd",
                grad_cscores_low,
                heads_of(cquery_low),
                preferred_element_type=jnp.float32,
            )
            * scaling
        )
        .reshape(captions, PATCH, D)
        .astype(jnp.bfloat16)
    )
    grad_w_cquery = weight_grad(cross_in, grad_cquery)
    grad_b_cquery = bias_grad(grad_cquery)
    key_term = weight_grad(vision_low, grad_ckey)
    value_term = weight_grad(vision_low, grad_cvalue)
    value_bias_term = bias_grad(grad_cvalue)
    rows_grad = project_back(grad_ckey, back_ckey) + project_back(grad_cvalue, back_cvalue)
    unused_feats, grad_gain_vision, grad_shift_vision = vision_back(rows_grad)
    grad_first = jnp.concatenate(
        [grad_two_in + project_back(grad_cquery, back_cquery), grad_joined[:, NQ:]], axis=1
    )
    grad_one_in, grad_gain_one, grad_shift_one = norm_back_one(grad_first)
    grad_branch = grad_one_in.astype(jnp.bfloat16)
    grad_w_out = weight_grad(mixed_low, grad_branch)
    grad_b_out = bias_grad(grad_branch)
    grad_mixed = heads_of(project_back(grad_branch, back_out).astype(jnp.bfloat16))
    grad_probs = jnp.einsum(
        "cqhd,ckhd->chqk", grad_mixed, heads_of(value_low), preferred_element_type=jnp.float32
    )
    grad_value = (
        jnp.einsum("chqk,cqhd->ckhd", probs_low, grad_mixed, preferred_element_type=jnp.float32)
        .reshape(captions, SEQ, D)
        .astype(jnp.bfloat16)
    )
    (grad_scores,) = soft_back(grad_probs)
    grad_scores_low = grad_scores.astype(jnp.bfloat16)
    grad_query = (
        (
            jnp.einsum(
                "chqk,ckhd->cqhd",
                grad_scores_low,
                heads_of(key_low),
                preferred_element_type=jnp.float32,
            )
            * scaling
        )
        .reshape(captions, SEQ, D)
        .astype(jnp.bfloat16)
    )
    grad_key = (
        (
            jnp.einsum(
                "chqk,cqhd->ckhd",
                grad_scores_low,
                heads_of(query_low),
                preferred_element_type=jnp.float32,
            )
            * scaling
        )
        .reshape(captions, SEQ, D)
        .astype(jnp.bfloat16)
    )
    grad_w_query = weight_grad(hidden, grad_query)
    grad_b_query = bias_grad(grad_query)
    grad_w_key = weight_grad(hidden, grad_key)
    grad_w_value = weight_grad(hidden, grad_value)
    grad_b_value = bias_grad(grad_value)
    input_grad = (
        grad_one_in
        + project_back(grad_query, back_query)
        + project_back(grad_key, back_key)
        + project_back(grad_value, back_value)
    )
    owned = (
        lax.psum_scatter(
            grad_w_query.astype(jnp.bfloat16), "fsdp", scatter_dimension=0, tiled=True
        ).astype(jnp.float32),
        lax.psum_scatter(
            grad_b_query.astype(jnp.bfloat16), "fsdp", scatter_dimension=0, tiled=True
        ).astype(jnp.float32),
        lax.psum_scatter(
            grad_w_key.astype(jnp.bfloat16), "fsdp", scatter_dimension=0, tiled=True
        ).astype(jnp.float32),
        lax.psum_scatter(
            grad_w_value.astype(jnp.bfloat16), "fsdp", scatter_dimension=0, tiled=True
        ).astype(jnp.float32),
        lax.psum_scatter(
            grad_b_value.astype(jnp.bfloat16), "fsdp", scatter_dimension=0, tiled=True
        ).astype(jnp.float32),
        lax.psum_scatter(
            grad_w_out.astype(jnp.bfloat16), "fsdp", scatter_dimension=0, tiled=True
        ).astype(jnp.float32),
        lax.psum_scatter(
            grad_b_out.astype(jnp.bfloat16), "fsdp", scatter_dimension=0, tiled=True
        ).astype(jnp.float32),
        lax.psum_scatter(
            grad_gain_one.astype(jnp.bfloat16), "fsdp", scatter_dimension=0, tiled=True
        ).astype(jnp.float32),
        lax.psum_scatter(
            grad_shift_one.astype(jnp.bfloat16), "fsdp", scatter_dimension=0, tiled=True
        ).astype(jnp.float32),
        lax.psum_scatter(
            grad_w_cquery.astype(jnp.bfloat16), "fsdp", scatter_dimension=0, tiled=True
        ).astype(jnp.float32),
        lax.psum_scatter(
            grad_b_cquery.astype(jnp.bfloat16), "fsdp", scatter_dimension=0, tiled=True
        ).astype(jnp.float32),
        lax.psum_scatter(
            key_term.astype(jnp.bfloat16), "fsdp", scatter_dimension=0, tiled=True
        ).astype(jnp.float32),
        lax.psum_scatter(
            value_term.astype(jnp.bfloat16), "fsdp", scatter_dimension=0, tiled=True
        ).astype(jnp.float32),
        lax.psum_scatter(
            value_bias_term.astype(jnp.bfloat16), "fsdp", scatter_dimension=0, tiled=True
        ).astype(jnp.float32),
        lax.psum_scatter(
            grad_w_cout.astype(jnp.bfloat16), "fsdp", scatter_dimension=0, tiled=True
        ).astype(jnp.float32),
        lax.psum_scatter(
            grad_b_cout.astype(jnp.bfloat16), "fsdp", scatter_dimension=0, tiled=True
        ).astype(jnp.float32),
        lax.psum_scatter(
            grad_gain_two.astype(jnp.bfloat16), "fsdp", scatter_dimension=0, tiled=True
        ).astype(jnp.float32),
        lax.psum_scatter(
            grad_shift_two.astype(jnp.bfloat16), "fsdp", scatter_dimension=0, tiled=True
        ).astype(jnp.float32),
        lax.psum_scatter(
            grad_gain_vision.astype(jnp.bfloat16), "fsdp", scatter_dimension=0, tiled=True
        ).astype(jnp.float32),
        lax.psum_scatter(
            grad_shift_vision.astype(jnp.bfloat16), "fsdp", scatter_dimension=0, tiled=True
        ).astype(jnp.float32),
        lax.psum_scatter(
            grad_w_expand.astype(jnp.bfloat16), "fsdp", scatter_dimension=1, tiled=True
        ).astype(jnp.float32),
        lax.psum_scatter(
            grad_b_expand.astype(jnp.bfloat16), "fsdp", scatter_dimension=0, tiled=True
        ).astype(jnp.float32),
        lax.psum_scatter(
            grad_w_contract.astype(jnp.bfloat16), "fsdp", scatter_dimension=0, tiled=True
        ).astype(jnp.float32),
        lax.psum_scatter(
            grad_b_contract.astype(jnp.bfloat16), "fsdp", scatter_dimension=0, tiled=True
        ).astype(jnp.float32),
        lax.psum_scatter(
            grad_gain_three.astype(jnp.bfloat16), "fsdp", scatter_dimension=0, tiled=True
        ).astype(jnp.float32),
        lax.psum_scatter(
            grad_shift_three.astype(jnp.bfloat16), "fsdp", scatter_dimension=0, tiled=True
        ).astype(jnp.float32),
    )
    summed = (
        lax.psum(owned[0].astype(jnp.bfloat16), "dp").astype(jnp.float32),
        lax.psum(owned[1].astype(jnp.bfloat16), "dp").astype(jnp.float32),
        lax.psum(owned[2].astype(jnp.bfloat16), "dp").astype(jnp.float32),
        lax.psum(owned[3].astype(jnp.bfloat16), "dp").astype(jnp.float32),
        lax.psum(owned[4].astype(jnp.bfloat16), "dp").astype(jnp.float32),
        lax.psum(owned[5].astype(jnp.bfloat16), "dp").astype(jnp.float32),
        lax.psum(owned[6].astype(jnp.bfloat16), "dp").astype(jnp.float32),
        lax.psum(owned[7].astype(jnp.bfloat16), "dp").astype(jnp.float32),
        lax.psum(owned[8].astype(jnp.bfloat16), "dp").astype(jnp.float32),
        lax.psum(owned[9].astype(jnp.bfloat16), "dp").astype(jnp.float32),
        lax.psum(owned[10].astype(jnp.bfloat16), "dp").astype(jnp.float32),
        lax.psum(owned[11].astype(jnp.bfloat16), "dp").astype(jnp.float32),
        lax.psum(owned[12].astype(jnp.bfloat16), "dp").astype(jnp.float32),
        lax.psum(owned[13].astype(jnp.bfloat16), "dp").astype(jnp.float32),
        lax.psum(owned[14].astype(jnp.bfloat16), "dp").astype(jnp.float32),
        lax.psum(owned[15].astype(jnp.bfloat16), "dp").astype(jnp.float32),
        lax.psum(owned[16].astype(jnp.bfloat16), "dp").astype(jnp.float32),
        lax.psum(owned[17].astype(jnp.bfloat16), "dp").astype(jnp.float32),
        lax.psum(owned[18].astype(jnp.bfloat16), "dp").astype(jnp.float32),
        lax.psum(owned[19].astype(jnp.bfloat16), "dp").astype(jnp.float32),
        lax.psum(owned[20].astype(jnp.bfloat16), "dp").astype(jnp.float32),
        lax.psum(owned[21].astype(jnp.bfloat16), "dp").astype(jnp.float32),
        lax.psum(owned[22].astype(jnp.bfloat16), "dp").astype(jnp.float32),
        lax.psum(owned[23].astype(jnp.bfloat16), "dp").astype(jnp.float32),
        lax.psum(owned[24].astype(jnp.bfloat16), "dp").astype(jnp.float32),
        lax.psum(owned[25].astype(jnp.bfloat16), "dp").astype(jnp.float32),
    )
    return (
        layer_out,
        input_grad,
        summed[0],
        summed[1],
        summed[2],
        summed[3],
        summed[4],
        summed[5],
        summed[6],
        summed[7],
        summed[8],
        summed[9],
        summed[10],
        summed[11],
        summed[12],
        summed[13],
        summed[14],
        summed[15],
        summed[16],
        summed[17],
        summed[18],
        summed[19],
        summed[20],
        summed[21],
        summed[22],
        summed[23],
        summed[24],
        summed[25],
    )


def solution(mesh):
    placed = (
        P(("dp", "fsdp"), None, None),
        P(("dp", "fsdp"), None, None),
        P(("dp", "fsdp"), None),
        P(("dp", "fsdp")),
        P(("dp", "fsdp"), None, None),
        P("fsdp", None),
        P("fsdp"),
        P("fsdp", None),
        P("fsdp", None),
        P("fsdp"),
        P("fsdp", None),
        P("fsdp"),
        P("fsdp"),
        P("fsdp"),
        P("fsdp", None),
        P("fsdp"),
        P("fsdp", None),
        P("fsdp", None),
        P("fsdp"),
        P("fsdp", None),
        P("fsdp"),
        P("fsdp"),
        P("fsdp"),
        P("fsdp"),
        P("fsdp"),
        P(None, "fsdp"),
        P("fsdp"),
        P("fsdp", None),
        P("fsdp"),
        P("fsdp"),
        P("fsdp"),
    )
    return jax.shard_map(
        local,
        mesh=mesh,
        in_specs=placed,
        out_specs=(
            P(("dp", "fsdp"), None, None),
            P(("dp", "fsdp"), None, None),
            P("fsdp", None),
            P("fsdp"),
            P("fsdp", None),
            P("fsdp", None),
            P("fsdp"),
            P("fsdp", None),
            P("fsdp"),
            P("fsdp"),
            P("fsdp"),
            P("fsdp", None),
            P("fsdp"),
            P("fsdp", None),
            P("fsdp", None),
            P("fsdp"),
            P("fsdp", None),
            P("fsdp"),
            P("fsdp"),
            P("fsdp"),
            P("fsdp"),
            P("fsdp"),
            P(None, "fsdp"),
            P("fsdp"),
            P("fsdp", None),
            P("fsdp"),
            P("fsdp"),
            P("fsdp"),
        ),
        check_vma=False,
    )
```

profile of v0, /device:TPU:0, one launch (start us, length us, event | category | flops | bytes accessed | tf_op | source)
XLA Modules:
  0.0 1431.0 jit_solution(11542918300369284845)
XLA Ops:
  28.5 39.1 %all-reduce.32 = (bf16[768]{0:T(1024)(128)(2,1)S(1)}, bf16[768]{0:T(1024)(128)(2,1)S(1)}, bf16[768]{0:T(1024)(128)(2,1)S(1)}, bf16[768]{0:T(1024)(128)(2,1)S(1)}...) all-reduce(bf16[768]{0:T(1024)(128)(2,1)S(1)} %dynamic-update-slice, ...), channel_id=1, replica_groups=mesh['dp'=4,'fsdp'=8] {'fsdp'}, use_global_device_ids=true, to_apply=%add | all-reduce | flops 12032 | bytes 48128
  68.5 4.1 fusion.107
  76.4 26.5 %all-gather = bf16[8,1,384]{2,1,0:T(2,128)(2,1)S(1)} all-gather(bf16[1,1,384]{2,1,0:T(2,128)(2,1)S(1)} %reshape.420), channel_id=1, replica_groups=mesh['dp'=4,'fsdp'=8] {'fsdp'}, dimensions={0}, use_global_device_ids=true | all-gather | bytes 6912 | tf_op jit(solution)/shard_map/all_gather | solution.py:116
  104.2 4.1 add_convert_fusion
  120.4 18.0 %all-gather.12.cloned.1.call-done = bf16[768,768]{1,0:T(8,128)(2,1)} async-done(((bf16[96,768]{1,0:T(8,128)(2,1)}), bf16[768,768]{1,0:T(8,128)(2,1)}) %all-gather.12.cloned.1.call-update) | async-done | bytes 1179664 | tf_op jit(solution)/shard_map/all_gather | solution.py:98
  141.3 3.9 reshape.365
  152.9 27.3 %all-gather.18.cloned.1.call-done = bf16[768,768]{1,0:T(8,128)(2,1)} async-done(((bf16[96,768]{1,0:T(8,128)(2,1)}), bf16[768,768]{1,0:T(8,128)(2,1)}) %all-gather.18.cloned.1.call-update) | async-done | bytes 1179664 | tf_op jit(solution)/shard_map/all_gather | solution.py:100
  185.7 36.4 %all-gather.22.cloned.1.call-done = bf16[768,768]{1,0:T(8,128)(2,1)} async-done(((bf16[96,768]{1,0:T(8,128)(2,1)}), bf16[768,768]{1,0:T(8,128)(2,1)}) %all-gather.22.cloned.1.call-update) | async-done | bytes 1179664 | tf_op jit(solution)/shard_map/all_gather | solution.py:104
  224.8 48.2 %all-gather.20.cloned.1.call-done = bf16[1408,768]{1,0:T(8,128)(2,1)} async-done(((bf16[176,768]{1,0:T(8,128)(2,1)}), bf16[1408,768]{1,0:T(8,128)(2,1)}) %all-gather.20.cloned.1.call-update) | async-done | bytes 2162704 | tf_op jit(solution)/shard_map/all_gather | solution.py:107
  273.0 10.6 add_convert_fusion.1
  283.6 40.0 %all-gather.24.cloned.1.call-done = bf16[1408,768]{1,0:T(8,128)(2,1)} async-done(((bf16[176,768]{1,0:T(8,128)(2,1)}), bf16[1408,768]{1,0:T(8,128)(2,1)}) %all-gather.24.cloned.1.call-update) | async-done | bytes 2162704 | tf_op jit(solution)/shard_map/all_gather | solution.py:106
  323.6 10.9 fusion.24
  334.5 6.2 copy.180
  340.7 6.2 copy.178
  355.2 10.2 all-gather.26.cloned.1.call-done
  369.5 77.8 %all-gather.28.cloned.1.call-done = bf16[768,3072]{1,0:T(8,128)(2,1)} async-done(((bf16[768,384]{1,0:T(8,128)(2,1)}), bf16[768,3072]{1,0:T(8,128)(2,1)}) %all-gather.28.cloned.1.call-update) | async-done | bytes 4718608 | tf_op jit(solution)/shard_map/all_gather | solution.py:115
  447.3 6.5 fusion.42
  456.4 15.8 %multiply_convert_fusion.1 = (bf16[8,64,3072]{2,1,0:T(8,128)(2,1)}, f32[8,64,3072]{2,1,0:T(8,128)}) fusion(f32[8,64,3072]{2,1,0:T(8,128)S(1)} %get-tuple-element.251, f32[3072]{0:T(1024)S(1)} %bitcast.205, u8[64,3072]{1,0:T(8,128)(4,1)S(1)} %get-tuple-element.143, u8[64,3072]{1,0:T(8,128)(4,1)S(1)} %get-tuple-element.142), kind=kLoop, calls=%fused_computation.16 | loop fusion | flops 111673344 | bytes 16134144 | tf_op jit(solution)/shard_map/convert_element_type | solution.py:224
  472.2 55.2 %all-gather.30.cloned.1.call-done = bf16[3072,768]{1,0:T(8,128)(2,1)} async-done(((bf16[384,768]{1,0:T(8,128)(2,1)}), bf16[3072,768]{1,0:T(8,128)(2,1)}) %all-gather.30.cloned.1.call-update) | async-done | bytes 4718608 | tf_op jit(solution)/shard_map/all_gather | solution.py:117
  527.5 6.5 fusion.109
  537.3 9.1 fusion.115
  546.4 6.1 add_add_fusion.5
  557.8 7.8 convert_reduce_fusion
  570.0 4.8 fusion.113
  591.3 5.1 convert_reduce_fusion.1
  611.6 4.6 fusion.111
  638.6 6.3 bitcast_convert_fusion.1
  644.8 6.7 copy.226
  657.9 6.3 multiply_convert_fusion
  664.2 6.7 copy.198
  672.5 10.4 bitcast_convert_fusion.3
  682.9 6.5 fusion.114
  689.4 5.4 copy.200
  695.1 12.1 bitcast_convert_fusion.2
  707.3 6.9 bitcast_convert_fusion
  717.3 10.1 fusion.27
  727.5 9.9 fusion.95
  737.5 35.2 %all-reduce.31 = (bf16[768]{0:T(1024)(128)(2,1)S(1)}, bf16[768]{0:T(1024)(128)(2,1)S(1)}, bf16[768]{0:T(1024)(128)(2,1)S(1)}, bf16[768]{0:T(1024)(128)(2,1)S(1)}...) all-reduce(bf16[768]{0:T(1024)(128)(2,1)S(1)} %dynamic-update-slice, ...), channel_id=1, replica_groups=mesh['dp'=4,'fsdp'=8] {'fsdp'}, use_global_device_ids=true, to_apply=%add.14 | all-reduce | flops 16640 | bytes 66560
  774.0 6.1 all-reduce.33
  791.9 15.0 %reduce-scatter.31.cloned.1.call-done = bf16[96,768]{1,0:T(8,128)(2,1)} async-done(((bf16[768,768]{1,0:T(8,128)(2,1)}), bf16[96,768]{1,0:T(8,128)(2,1)}) %reduce-scatter.31.cloned.1.call-update) | async-done | bytes 147472
  808.7 96.0 %reduce-scatter.37.cloned.1.call-done = bf16[384,768]{1,0:T(8,128)(2,1)} async-done(((bf16[3072,768]{1,0:T(8,128)(2,1)}), bf16[384,768]{1,0:T(8,128)(2,1)}) %reduce-scatter.37.cloned.1.call-update) | async-done | bytes 589840
  906.8 64.9 %reduce-scatter.27.cloned.1.call-done = bf16[96,768]{1,0:T(8,128)(2,1)} async-done(((bf16[768,768]{1,0:T(8,128)(2,1)}), bf16[96,768]{1,0:T(8,128)(2,1)}) %reduce-scatter.27.cloned.1.call-update) | async-done | bytes 147472 | tf_op jit(solution)/shard_map/reduce_scatter | solution.py:408
  971.8 66.5 %reduce-scatter.19.cloned.1.call-done = bf16[96,768]{1,0:T(8,128)(2,1)} async-done(((bf16[768,768]{1,0:T(8,128)(2,1)}), bf16[96,768]{1,0:T(8,128)(2,1)}) %reduce-scatter.19.cloned.1.call-update) | async-done | bytes 147472 | tf_op jit(solution)/shard_map/reduce_scatter | solution.py:381
  1038.3 66.9 %reduce-scatter.21.cloned.1.call-done = bf16[96,768]{1,0:T(8,128)(2,1)} async-done(((bf16[768,768]{1,0:T(8,128)(2,1)}), bf16[96,768]{1,0:T(8,128)(2,1)}) %reduce-scatter.21.cloned.1.call-update) | async-done | bytes 147472 | tf_op jit(solution)/shard_map/reduce_scatter | solution.py:393
  1105.2 71.0 %reduce-scatter.23.cloned.1.call-done = bf16[176,768]{1,0:T(8,128)(2,1)} async-done(((bf16[1408,768]{1,0:T(8,128)(2,1)}), bf16[176,768]{1,0:T(8,128)(2,1)}) %reduce-scatter.23.cloned.1.call-update) | async-done | bytes 270352 | tf_op jit(solution)/shard_map/reduce_scatter | solution.py:399
  1176.2 70.8 %reduce-scatter.25.cloned.1.call-done = bf16[176,768]{1,0:T(8,128)(2,1)} async-done(((bf16[1408,768]{1,0:T(8,128)(2,1)}), bf16[176,768]{1,0:T(8,128)(2,1)}) %reduce-scatter.25.cloned.1.call-update) | async-done | bytes 270352 | tf_op jit(solution)/shard_map/reduce_scatter | solution.py:402
  1246.9 97.7 %reduce-scatter.29.cloned.1.call-done = bf16[384,768]{1,0:T(8,128)(2,1)} async-done(((bf16[3072,768]{1,0:T(8,128)(2,1)}), bf16[384,768]{1,0:T(8,128)(2,1)}) %reduce-scatter.29.cloned.1.call-update) | async-done | bytes 589840 | tf_op jit(solution)/shard_map/reduce_scatter | solution.py:432
  1350.2 62.7 %all-reduce.37.cloned.1.call-done = (bf16[96,768]{0,1:T(8,128)(2,1)}, bf16[96,768]{0,1:T(8,128)(2,1)}, bf16[96,768]{0,1:T(8,128)(2,1)}, bf16[96,768]{1,0:T(8,128...) async-done(((bf16[96,768]{0,1:T(8,128)(2,1)}, ...) | async-done | bytes 2605072 | tf_op jit(solution)/shard_map/psum | solution.py:446
  (478 shorter events, 179.9 us)
Async XLA Ops:
  7.2 61.3 %copy-start = (bf16[3,257,1408]{2,1,0:T(8,128)(2,1)S(1)}, bf16[3,257,1408]{2,1,0:T(8,128)(2,1)}, u32[]{:S(2)}) copy-start(bf16[3,257,1408]{2,1,0:T(8,128)(2,1)} %param.32) | copy-start | bytes 6513412
  7.2 101.1 %all-gather.14.cloned.1.call-start = ((), (), s32[]{:S(2)}) async-start(), calls=%async_computation.11 | async-start | bytes 1327104 | tf_op jit(solution)/shard_map/all_gather | solution.py:95
  8.0 105.1 %all-gather.16.cloned.1.call-start = ((), (), s32[]{:S(2)}) async-start(), calls=%async_computation.12 | async-start | bytes 1327104 | tf_op jit(solution)/shard_map/all_gather | solution.py:97
  8.7 129.7 %all-gather.12.cloned.1.call-start = ((), (), s32[]{:S(2)}) async-start(), calls=%async_computation.10 | async-start | bytes 1327104 | tf_op jit(solution)/shard_map/all_gather | solution.py:98
  9.4 170.8 %all-gather.18.cloned.1.call-start = ((), (), s32[]{:S(2)}) async-start(), calls=%async_computation.13 | async-start | bytes 1327104 | tf_op jit(solution)/shard_map/all_gather | solution.py:100
  10.0 212.2 %all-gather.22.cloned.1.call-start = ((), (), s32[]{:S(2)}) async-start(), calls=%async_computation.15 | async-start | bytes 1327104 | tf_op jit(solution)/shard_map/all_gather | solution.py:104
  10.6 262.4 %all-gather.20.cloned.1.call-start = ((), (), s32[]{:S(2)}) async-start(), calls=%async_computation.14 | async-start | bytes 2433024 | tf_op jit(solution)/shard_map/all_gather | solution.py:107
  11.2 312.5 %all-gather.24.cloned.1.call-start = ((), (), s32[]{:S(2)}) async-start(), calls=%async_computation.16 | async-start | bytes 2433024 | tf_op jit(solution)/shard_map/all_gather | solution.py:106
  11.9 353.5 %all-gather.26.cloned.1.call-start = ((), (), s32[]{:S(2)}) async-start(), calls=%async_computation.17 | async-start | bytes 1327104 | tf_op jit(solution)/shard_map/all_gather | solution.py:109
  12.7 434.6 %all-gather.28.cloned.1.call-start = ((), (), s32[]{:S(2)}) async-start(), calls=%async_computation.18 | async-start | bytes 5308416 | tf_op jit(solution)/shard_map/all_gather | solution.py:115
  13.4 514.0 %all-gather.30.cloned.1.call-start = ((), (), s32[]{:S(2)}) async-start(), calls=%async_computation.19 | async-start | bytes 5308416 | tf_op jit(solution)/shard_map/all_gather | solution.py:117
  14.0 774.5 %reduce-scatter.33.cloned.1.call-start = ((), (), s32[]{:S(2)}) async-start(), calls=%async_computation.27 | async-start | bytes 1327104
  72.6 31.5 %copy-start.2 = (f32[8,257,1408]{2,0,1:T(8,128)}, f32[8,257,1408]{2,0,1:T(8,128)S(1)}, u32[]{:S(2)}) copy-start(f32[8,257,1408]{2,0,1:T(8,128)S(1)} %get-tuple-element.246) | copy-start | bytes 34738180
  72.7 31.5 %copy-start.34 = (f32[8,257]{0,1:T(8,128)}, f32[8,257]{0,1:T(8,128)S(1)}, u32[]{:S(2)}) copy-start(f32[8,257]{0,1:T(8,128)S(1)} %broadcast_multiply_fusion) | copy-start | bytes 24676
  72.7 31.4 %copy-start.106 = (s32[8]{0:T(128)S(1)}, s32[8]{0:T(128)}, u32[]{:S(2)}) copy-start(s32[8]{0:T(128)} %param.34) | copy-start | bytes 100
  74.0 30.1 %copy-start.61 = (f32[8,257]{0,1:T(8,128)}, f32[8,257]{0,1:T(8,128)S(1)}, u32[]{:S(2)}) copy-start(f32[8,257]{0,1:T(8,128)S(1)} %add_rsqrt_fusion) | copy-start | bytes 24676
  104.1 442.3 %copy-start.71 = (f32[768]{0:T(1024)}, f32[768]{0:T(1024)S(1)}, u32[]{:S(2)}) copy-start(f32[768]{0:T(1024)S(1)} %convert_element_type.449) | copy-start | bytes 9220
  104.2 45.3 %copy-start.91 = (pred[8,64]{1,0:T(8,128)(4,1)}, pred[8,64]{1,0:T(8,128)(4,1)S(1)}, u32[]{:S(2)}) copy-start(pred[8,64]{1,0:T(8,128)(4,1)S(1)} %compare_or_fusion) | copy-start | bytes 1540
  113.1 32.2 %copy-start.12 = (bf16[8,64,768]{1,2,0:T(8,128)(2,1)}, bf16[8,64,768]{1,2,0:T(8,128)(2,1)S(1)}, u32[]{:S(2)}) copy-start(bf16[8,64,768]{1,2,0:T(8,128)(2,1)S(1)} %copy.228) | copy-start | bytes 2359300
  183.3 38.9 %copy-start.83 = (f32[8,64]{1,0:T(8,128)}, f32[8,64]{1,0:T(8,128)S(1)}, u32[]{:S(2)}) copy-start(f32[8,64]{1,0:T(8,128)S(1)} %multiply_reduce_fusion.8) | copy-start | bytes 6148
  183.3 38.8 %copy-start.78 = (f32[8,64]{1,0:T(8,128)}, f32[8,64]{1,0:T(8,128)S(1)}, u32[]{:S(2)}) copy-start(f32[8,64]{1,0:T(8,128)S(1)} %fusion.86) | copy-start | bytes 6148
  224.8 122.2 %copy-start.20 = (bf16[8,32,12,64]{3,2,1,0:T(8,128)(2,1)}, bf16[8,32,12,64]{3,2,1,0:T(8,128)(2,1)S(1)}, u32[]{:S(2)}) copy-start(bf16[8,32,12,64]{3,2,1,0:T(8,128)(2,1)S(1)} %reshape.371) | copy-start | bytes 1179652
  351.9 15.8 %copy-start.56 = (f32[8,12,32]{2,1,0:T(8,128)}, f32[8,12,32]{2,1,0:T(8,128)S(1)}, u32[]{:S(2)}) copy-start(f32[8,12,32]{2,1,0:T(8,128)S(1)} %fusion.32) | copy-start | bytes 36868
  354.2 11.2 copy-start.90
  354.6 13.8 copy-start.89
  355.2 92.1 %copy-start.80 = (f32[8,1,384]{2,1,0:T(1,128)S(1)}, f32[8,1,384]{2,1,0:T(1,128)}, u32[]{:S(2)}) copy-start(f32[8,1,384]{2,1,0:T(1,128)} %convert_element_type.526) | copy-start | bytes 36868
  456.4 71.1 %copy-start.103 = (f32[768]{0:T(1024)S(1)}, f32[768]{0:T(1024)}, u32[]{:S(2)}) copy-start(f32[768]{0:T(1024)} %convert_element_type.448) | copy-start | bytes 9220
  534.0 12.4 copy-start.8
  534.0 12.4 copy-start.73
  534.5 11.9 copy-start.75
  611.1 179.1 %reduce-scatter.35.cloned.1.call-start = ((), (), s32[]{:S(2)}) async-start(), calls=%async_computation.28 | async-start | bytes 1327104
  628.1 178.8 %reduce-scatter.31.cloned.1.call-start = ((), (), s32[]{:S(2)}) async-start(), calls=%async_computation.26 | async-start | bytes 1327104
  638.5 266.2 %reduce-scatter.37.cloned.1.call-start = ((), (), s32[]{:S(2)}) async-start(), calls=%async_computation.29 | async-start | bytes 5308416
  651.5 320.3 %reduce-scatter.27.cloned.1.call-start = ((), (), s32[]{:S(2)}) async-start(), calls=%async_computation.24 | async-start | bytes 1327104 | tf_op jit(solution)/shard_map/reduce_scatter | solution.py:408
  654.1 384.2 %reduce-scatter.19.cloned.1.call-start = ((), (), s32[]{:S(2)}) async-start(), calls=%async_computation.20 | async-start | bytes 1327104 | tf_op jit(solution)/shard_map/reduce_scatter | solution.py:381
  657.6 447.6 %reduce-scatter.21.cloned.1.call-start = ((), (), s32[]{:S(2)}) async-start(), calls=%async_computation.21 | async-start | bytes 1327104 | tf_op jit(solution)/shard_map/reduce_scatter | solution.py:393
  672.4 503.7 %reduce-scatter.23.cloned.1.call-start = ((), (), s32[]{:S(2)}) async-start(), calls=%async_computation.22 | async-start | bytes 2433024 | tf_op jit(solution)/shard_map/reduce_scatter | solution.py:399
  694.8 12.4 copy-start.26
  694.8 552.1 %reduce-scatter.25.cloned.1.call-start = ((), (), s32[]{:S(2)}) async-start(), calls=%async_computation.23 | async-start | bytes 2433024 | tf_op jit(solution)/shard_map/reduce_scatter | solution.py:402
  707.3 637.4 %reduce-scatter.29.cloned.1.call-start = ((), (), s32[]{:S(2)}) async-start(), calls=%async_computation.25 | async-start | bytes 5308416 | tf_op jit(solution)/shard_map/reduce_scatter | solution.py:432
  714.3 13.1 slice-start
  714.3 698.6 %all-reduce.37.cloned.1.call-start = ((), (), s32[]{:S(2)}) async-start(), calls=%async_computation.30 | async-start | bytes 5505024 | tf_op jit(solution)/shard_map/psum | solution.py:446
  737.4 607.3 %copy-start.9 = (f32[8,64,768]{2,1,0:T(8,128)S(1)}, f32[8,64,768]{2,1,0:T(8,128)}, u32[]{:S(2)}) copy-start(f32[8,64,768]{2,1,0:T(8,128)} %copy-done.8) | copy-start | bytes 4718596
  737.4 607.3 %copy-start.72 = (f32[768]{0:T(1024)S(1)}, f32[768]{0:T(1024)}, u32[]{:S(2)}) copy-start(f32[768]{0:T(1024)} %copy-done.71) | copy-start | bytes 9220
  737.4 607.3 %copy-start.74 = (f32[8,64]{1,0:T(8,128)S(1)}, f32[8,64]{1,0:T(8,128)}, u32[]{:S(2)}) copy-start(f32[8,64]{1,0:T(8,128)} %copy-done.73) | copy-start | bytes 6148
  737.4 607.3 %copy-start.76 = (f32[8,64]{1,0:T(8,128)S(1)}, f32[8,64]{1,0:T(8,128)}, u32[]{:S(2)}) copy-start(f32[8,64]{1,0:T(8,128)} %copy-done.75) | copy-start | bytes 6148
  906.8 439.3 %copy-start.43 = (bf16[8,64,768]{2,1,0:T(8,128)(2,1)S(1)}, bf16[8,64,768]{2,1,0:T(8,128)(2,1)}, u32[]{:S(2)}) copy-start(bf16[8,64,768]{2,1,0:T(8,128)(2,1)} %convert_element_type.470) | copy-start | bytes 2359300
  906.8 439.3 %copy-start.108 = (bf16[768,768]{1,0:T(8,128)(2,1)S(1)}, bf16[768,768]{1,0:T(8,128)(2,1)}, u32[]{:S(2)}) copy-start(bf16[768,768]{1,0:T(8,128)(2,1)} %all-gather.16.cloned.1.call-done) | copy-start | bytes 3538948
  (94 other events, 505.1 us)
Sparse Core Ops, SparseCore 0:
  10.2 43.9 all-gather.13
  56.5 39.8 all-gather.15
  98.5 39.8 all-gather.11
  140.4 39.8 all-gather.17
  182.3 39.8 all-gather.21
  224.2 48.7 all-gather.19
  275.1 48.4 all-gather.23
  325.8 39.5 all-gather.25
  367.5 79.7 all-gather.27
  449.3 78.0 all-gather.29
  611.3 62.1 reduce-scatter.32
  676.7 63.0 reduce-scatter.34
  743.7 63.1 reduce-scatter.30
  810.5 94.2 reduce-scatter.36
  907.9 63.7 reduce-scatter.26
  975.0 63.1 reduce-scatter.18
  1042.1 63.0 reduce-scatter.20
  1108.5 67.5 reduce-scatter.22
  1179.6 67.2 reduce-scatter.24
  1250.4 94.1 reduce-scatter.28
  1349.5 63.4 all-reduce.36
where the time goes:
time: 1440 us; the launch traced here: 1430 us
  waiting for transfers between devices  931 us (65%)
  matrix products  199 us (14%)
  local copies, waits for them, and re-layouts  108 us (8%)
  blocking collectives  107 us (7%)
  other arithmetic  63.9 us (4%)
  between operations  19.9 us (1%)
    unnamed x25, waiting for transfers between devices  117 us
    reduce_scatter x1, waiting for transfers between devices, local(): lax.psum_scatter(grad_w_contract.astype(jnp.bfloat16), 'fsdp', scatter_di...  97.7 us
    all_gather x1, waiting for transfers between devices, local(): lax.all_gather(expand_weight, 'fsdp', axis=1, tiled=True)  77.8 us
    unnamed x2, blocking collectives  74.3 us
    reduce_scatter x1, waiting for transfers between devices, local(): lax.psum_scatter(key_term.astype(jnp.bfloat16), 'fsdp', scatter_dimension...  71 us
    reduce_scatter x1, waiting for transfers between devices, local(): lax.psum_scatter(value_term.astype(jnp.bfloat16), 'fsdp', scatter_dimensi...  70.8 us
    reduce_scatter x1, waiting for transfers between devices, local(): lax.psum_scatter(grad_w_cquery.astype(jnp.bfloat16), 'fsdp', scatter_dime...  66.9 us
    reduce_scatter x1, waiting for transfers between devices, local(): lax.psum_scatter(grad_w_out.astype(jnp.bfloat16), 'fsdp', scatter_dimensi...  66.5 us
  transfers between devices with their start and end apart: 21, of which 17 were waited for; matrix products, arithmetic and copies ran while one was open for 19% of the time, Pallas kernels for 0%

commit v1 on v0

v1 whole, which is shorter than its diff:
```python
import functools

import jax
import jax.numpy as jnp
from jax import lax
from jax.experimental import pallas as pl
from jax.experimental.pallas import tpu as pltpu
from jax.sharding import PartitionSpec as P

D = 768
HEADS = 12
HDIM = 64
PATCH = 257
NQ = 32
SEQ = 64
EPS = 1e-06
MASKED = -1000000000.0


def norm_rows(values, gain_row, shift_row):
    center = values - jnp.mean(values, axis=-1, keepdims=True)
    spread = jnp.mean(center * center, axis=-1, keepdims=True)
    return center * lax.rsqrt(spread + EPS) * gain_row + shift_row


def softmax_rows(scores):
    row_top = jnp.max(scores, axis=-1, keepdims=True)
    shifted = jnp.exp(scores - row_top)
    return shifted / jnp.sum(shifted, axis=-1, keepdims=True)


def gelu_exact(values):
    return jax.nn.gelu(values, approximate=False)


def project(operand, weight):
    return jnp.einsum("...k,kn->...n", operand, weight, preferred_element_type=jnp.float32)


def project_back(upstream, weight):
    return jnp.einsum("...n,kn->...k", upstream, weight, preferred_element_type=jnp.float32)


def weight_grad(operand, upstream):
    flat_operand = operand.reshape(-1, operand.shape[-1])
    flat_upstream = upstream.reshape(-1, upstream.shape[-1])
    return lax.dot_general(
        flat_operand, flat_upstream, (((0,), (0,)), ((), ())), preferred_element_type=jnp.float32
    )


def bias_grad(upstream):
    return jnp.sum(upstream.reshape(-1, upstream.shape[-1]), axis=0, dtype=jnp.float32)


def heads_of(values):
    return values.reshape(values.shape[:-1] + (HEADS, HDIM))


def as_float(values):
    return values.astype(jnp.float32)


MESH = pl.DeviceIdType.MESH
COMM_VMEM = 56 * 1024 * 1024


def place():
    dp, fs = lax.axis_index("dp"), lax.axis_index("fsdp")
    return dp // 2, dp % 2, fs // 2, fs % 2


def at_device(y, c, z, x):
    return (2 * y + c, 2 * z + x)


def rows_at(start, size):
    return pl.ds(pl.multiple_of(start, 16), size)


def greet(peers):
    barrier = pltpu.get_barrier_semaphore()
    for peer in peers:
        pl.semaphore_signal(barrier, inc=1, device_id=peer, device_id_type=MESH)
    pl.semaphore_wait(barrier, len(peers))


class Piece:
    def __init__(self, array, four, size, which, start):
        self.array, self.four, self.size, self.which, self.start = array, four, size, which, start

    def shard(self, refs, y, c):
        return refs[self.array].at[self.which(y, c), rows_at(self.start(y, c), self.size)]

    def at(self, refs, y, c, z, x):
        return refs[self.array].at[self.which(y, c), z, x, rows_at(self.start(y, c), self.size)]

    def column(self, refs, y, c, x):
        return refs[self.array].at[self.which(y, c), :, x, rows_at(self.start(y, c), self.size)]

    def every(self, refs, y, c):
        return refs[self.array].at[self.which(y, c), :, :, rows_at(self.start(y, c), self.size)]


ARRAY_ROWS = ((1, 32), (4, 96), (2, 176), (2, 96), (1, 384), (1, 384))
GATHER_PIECES = (
    Piece(0, False, 16, lambda y, c: 0, lambda y, c: 16 * c),
    Piece(1, True, 96, lambda y, c: 2 * y + c, lambda y, c: 0),
    Piece(2, True, 80, lambda y, c: y, lambda y, c: 80 * c),
    Piece(2, False, 16, lambda y, c: c, lambda y, c: 160),
    Piece(3, True, 48, lambda y, c: y, lambda y, c: 48 * c),
    Piece(4, True, 48, lambda y, c: 0, lambda y, c: 48 * (2 * y + c)),
    Piece(4, False, 96, lambda y, c: 0, lambda y, c: 192 + 96 * c),
    Piece(5, True, 48, lambda y, c: 0, lambda y, c: 48 * (2 * y + c)),
    Piece(5, False, 96, lambda y, c: 0, lambda y, c: 192 + 96 * c),
)
SUM_PIECES = (
    Piece(5, True, 48, lambda y, c: 0, lambda y, c: 48 * (2 * y + c)),
    Piece(5, False, 96, lambda y, c: 0, lambda y, c: 192 + 96 * c),
    Piece(4, True, 48, lambda y, c: 0, lambda y, c: 48 * (2 * y + c)),
    Piece(4, False, 96, lambda y, c: 0, lambda y, c: 192 + 96 * c),
    Piece(3, True, 32, lambda y, c: y, lambda y, c: 32 * c),
    Piece(3, False, 32, lambda y, c: c, lambda y, c: 64),
    Piece(2, True, 48, lambda y, c: y, lambda y, c: 48 * c),
    Piece(2, False, 80, lambda y, c: c, lambda y, c: 96),
    Piece(1, True, 48, lambda y, c: 2 * y + c, lambda y, c: 0),
    Piece(1, False, 48, lambda y, c: 2 * c, lambda y, c: 48),
    Piece(1, False, 48, lambda y, c: 2 * c + 1, lambda y, c: 48),
    Piece(0, False, 16, lambda y, c: 0, lambda y, c: 16 * c),
)


def remote(src, dst, send, recv, device):
    return pltpu.make_async_remote_copy(
        src_ref=src, dst_ref=dst, send_sem=send, recv_sem=recv, device_id=device, device_id_type=MESH
    )


def gather_kernel(*refs):
    count = len(ARRAY_ROWS)
    own, full = refs[:count], refs[count : 2 * count]
    here, zs, xs, ys, cs, zs_s, xs_s, ys_s, cs_s = refs[2 * count :]
    y, c, z, x = place()
    zp = [lax.rem(z + i, 4) for i in (1, 2, 3)]
    zm = [lax.rem(z + 4 - i, 4) for i in (1, 2, 3)]
    to_z = [at_device(y, c, p, x) for p in zp]
    to_x, to_y, to_c = at_device(y, c, z, 1 - x), at_device(1 - y, c, z, x), at_device(y, 1 - c, z, x)
    greet(to_z + [to_x, to_y, to_c])
    sent = []

    def go(*spec):
        copy = remote(*spec)
        copy.start()
        sent.append(copy)

    def arrived(dst, recv, send):
        remote(dst, dst, send, recv, to_x).wait_recv()

    locals_ = []
    for k, p in enumerate(GATHER_PIECES):
        for i in range(3):
            go(p.shard(own, y, c), p.at(full, y, c, z, x), zs_s.at[k, i], zs.at[k, i], to_z[i])
        go(p.shard(own, y, c), p.at(full, y, c, z, x), xs_s.at[k, 0], xs.at[k, 0], to_x)
        for j in range(2 if p.four else 1):
            yy = y if j == 0 else 1 - y
            copy = pltpu.make_async_copy(p.shard(own, yy, c), p.at(full, yy, c, z, x), here.at[k, j])
            copy.start()
            locals_.append(copy)
    for copy in locals_:
        copy.wait()

    def stage_x(k):
        p = GATHER_PIECES[k]
        for i in range(3):
            got = p.at(full, y, c, zm[i], x)
            arrived(got, zs.at[k, i], zs_s.at[k, i])
            go(got, got, xs_s.at[k, i + 1], xs.at[k, i + 1], to_x)

    def stage_y(k):
        p = GATHER_PIECES[k]
        arrived(p.at(full, y, c, z, 1 - x), xs.at[k, 0], xs_s.at[k, 0])
        for i in range(3):
            arrived(p.at(full, y, c, zm[i], 1 - x), xs.at[k, i + 1], xs_s.at[k, i + 1])
        if p.four:
            far = p.column(full, y, c, 1 - x)
            go(far, far, ys_s.at[k, 0], ys.at[k, 0], to_y)
            for i in range(3):
                near = p.at(full, y, c, zm[i], x)
                go(near, near, ys_s.at[k, i + 1], ys.at[k, i + 1], to_y)
        mine = p.every(full, y, c)
        go(mine, mine, cs_s.at[k, 0], cs.at[k, 0], to_c)

    def stage_c(k):
        p = GATHER_PIECES[k]
        if p.four:
            arrived(p.column(full, 1 - y, c, 1 - x), ys.at[k, 0], ys_s.at[k, 0])
            for i in range(3):
                arrived(p.at(full, 1 - y, c, zm[i], x), ys.at[k, i + 1], ys_s.at[k, i + 1])
            mine = p.every(full, 1 - y, c)
            go(mine, mine, cs_s.at[k, 1], cs.at[k, 1], to_c)

    def finish(k):
        p = GATHER_PIECES[k]
        arrived(p.every(full, y, 1 - c), cs.at[k, 0], cs_s.at[k, 0])
        if p.four:
            arrived(p.every(full, 1 - y, 1 - c), cs.at[k, 1], cs_s.at[k, 1])

    total = len(GATHER_PIECES)
    for t in range(total + 3):
        for lag, stage in enumerate((stage_x, stage_y, stage_c, finish)):
            if 0 <= t - lag < total:
                stage(t - lag)
    for copy in sent:
        copy.wait_send()


def gather_all(shards):
    total = len(GATHER_PIECES)
    return pl.pallas_call(
        gather_kernel,
        out_shape=[
            jax.ShapeDtypeStruct((count, 4, 2, rows, D), jnp.bfloat16) for count, rows in ARRAY_ROWS
        ],
        in_specs=[pl.BlockSpec(memory_space=pl.ANY)] * len(ARRAY_ROWS),
        out_specs=[pl.BlockSpec(memory_space=pl.ANY)] * len(ARRAY_ROWS),
        scratch_shapes=[
            pltpu.SemaphoreType.DMA((total, 2)),
            pltpu.SemaphoreType.DMA((total, 3)),
            pltpu.SemaphoreType.DMA((total, 4)),
            pltpu.SemaphoreType.DMA((total, 4)),
            pltpu.SemaphoreType.DMA((total, 2)),
            pltpu.SemaphoreType.DMA((total, 3)),
            pltpu.SemaphoreType.DMA((total, 4)),
            pltpu.SemaphoreType.DMA((total, 4)),
            pltpu.SemaphoreType.DMA((total, 2)),
        ],
        compiler_params=pltpu.CompilerParams(collective_id=0, has_side_effects=True),
        cost_estimate=pl.CostEstimate(flops=0, bytes_accessed=100_000_000, transcendentals=0),
    )(*shards)


def add_pieces(target, other, lead):
    def step(i, carry):
        target[i] = target[i] + other[i]
        return carry

    lax.fori_loop(0, lead, step, 0)


def sum_kernel(*refs):
    count, total = len(ARRAY_ROWS), len(SUM_PIECES)
    grads, outs = refs[:count], refs[count : 2 * count]
    refs = refs[2 * count :]
    mine, from_c, from_y, from_x, from_z, last = (refs[i * total : (i + 1) * total] for i in range(6))
    here, done, cs, ys, xs, zs, fs, cs_s, ys_s, xs_s, zs_s, fs_s = refs[6 * total :]
    y, c, z, x = place()
    zp = [lax.rem(z + i, 4) for i in (1, 2, 3)]
    to_z = [at_device(y, c, p, x) for p in zp]
    to_x, to_y, to_c = at_device(y, c, z, 1 - x), at_device(1 - y, c, z, x), at_device(y, 1 - c, z, x)
    to_d = at_device(1 - y, 1 - c, z, x)
    greet(to_z + [to_x, to_y, to_c, to_d])
    sent, stored = [], []

    def go(*spec):
        copy = remote(*spec)
        copy.start()
        sent.append(copy)

    def arrived(dst, recv, send):
        remote(dst, dst, send, recv, to_x).wait_recv()

    def sides(p):
        return (y, 1 - y) if p.four else (y,)

    local = []
    for k, p in enumerate(SUM_PIECES):
        for j, yy in enumerate(sides(p)):
            copy = pltpu.make_async_copy(p.every(grads, yy, c), mine[k].at[j], here.at[k, j])
            copy.start()
            local.append((k, copy))
            go(p.every(grads, yy, 1 - c), from_c[k].at[j], cs_s.at[k, j], cs.at[k, j], to_c)

    def stage_c(k):
        p = SUM_PIECES[k]
        for kk, copy in local:
            if kk == k:
                copy.wait()
        for j in reversed(range(len(sides(p)))):
            arrived(from_c[k].at[j], cs.at[k, j], cs_s.at[k, j])
            for i in range(4):
                for l in range(2):
                    mine[k][j, i, l] = mine[k][j, i, l] + from_c[k][j, i, l]
            if j == 1:
                go(mine[k].at[1], from_y[k], ys_s.at[k], ys.at[k], to_y)

    def stage_y(k):
        p = SUM_PIECES[k]
        if p.four:
            arrived(from_y[k], ys.at[k], ys_s.at[k])
            for i in range(4):
                for l in range(2):
                    mine[k][0, i, l] = mine[k][0, i, l] + from_y[k][i, l]
        go(mine[k].at[0, :, 1 - x], from_x[k], xs_s.at[k], xs.at[k], to_x)

    def stage_x(k):
        arrived(from_x[k], xs.at[k], xs_s.at[k])
        for i in range(4):
            from_x[k][i] = from_x[k][i] + mine[k][0, i, x]
        for i in range(3):
            go(from_x[k].at[zp[i]], from_z[k].at[i], zs_s.at[k, i], zs.at[k, i], to_z[i])

    def stage_z(k):
        p = SUM_PIECES[k]
        for i in range(3):
            arrived(from_z[k].at[i], zs.at[k, i], zs_s.at[k, i])
        value = from_x[k][z].astype(jnp.float32)
        for i in range(3):
            value = value + from_z[k][i].astype(jnp.float32)
        last[k][0] = value.astype(jnp.bfloat16)
        if p.four:
            go(last[k].at[0], last[k].at[1], fs_s.at[k, 0], fs.at[k, 0], to_y)
            go(last[k].at[0], last[k].at[2], fs_s.at[k, 1], fs.at[k, 1], to_c)
            go(last[k].at[0], last[k].at[3], fs_s.at[k, 2], fs.at[k, 2], to_d)
        else:
            go(last[k].at[0], last[k].at[1], fs_s.at[k, 0], fs.at[k, 0], to_y)

    def put(k, j, slot, yy, cc):
        copy = pltpu.make_async_copy(last[k].at[slot], SUM_PIECES[k].shard(outs, yy, cc), done.at[k, j])
        copy.start()
        stored.append(copy)

    def stage_f(k):
        p = SUM_PIECES[k]
        if p.four:
            put(k, 0, 0, y, c)
            for j, (yy, cc) in enumerate(((1 - y, c), (y, 1 - c), (1 - y, 1 - c))):
                arrived(last[k].at[j + 1], fs.at[k, j], fs_s.at[k, j])
                put(k, j + 1, j + 1, yy, cc)
        else:
            arrived(last[k].at[1], fs.at[k, 0], fs_s.at[k, 0])
            last[k][2] = last[k][0] + last[k][1]
            go(last[k].at[2], last[k].at[3], fs_s.at[k, 1], fs.at[k, 1], to_c)
            put(k, 0, 2, y, c)

    def stage_g(k):
        p = SUM_PIECES[k]
        if not p.four:
            arrived(last[k].at[3], fs.at[k, 1], fs_s.at[k, 1])
            put(k, 1, 3, y, 1 - c)

    stages = (stage_c, stage_y, stage_x, stage_z, stage_f, stage_g)
    for t in range(total + len(stages) - 1):
        for lag, stage in enumerate(stages):
            if 0 <= t - lag < total:
                stage(t - lag)
    for copy in sent:
        copy.wait_send()
    for copy in stored:
        copy.wait()


def sum_all(grads):
    total = len(SUM_PIECES)
    low = jnp.bfloat16
    sides = [2 if p.four else 1 for p in SUM_PIECES]
    sizes = [p.size for p in SUM_PIECES]
    dma = pltpu.SemaphoreType.DMA
    return pl.pallas_call(
        sum_kernel,
        out_shape=[jax.ShapeDtypeStruct((count, rows, D), low) for count, rows in ARRAY_ROWS],
        in_specs=[pl.BlockSpec(memory_space=pl.ANY)] * len(ARRAY_ROWS),
        out_specs=[pl.BlockSpec(memory_space=pl.ANY)] * len(ARRAY_ROWS),
        scratch_shapes=[pltpu.VMEM((s, 4, 2, n, D), low) for s, n in zip(sides, sizes)]
        + [pltpu.VMEM((s, 4, 2, n, D), low) for s, n in zip(sides, sizes)]
        + [pltpu.VMEM((4, 2, n, D) if s == 2 else (1, 1, 16, D), low) for s, n in zip(sides, sizes)]
        + [pltpu.VMEM((4, n, D), low) for n in sizes]
        + [pltpu.VMEM((3, n, D), low) for n in sizes]
        + [pltpu.VMEM((4, n, D), low) for n in sizes]
        + [
            dma((total, 2)),
            dma((total, 4)),
            dma((total, 2)),
            dma((total,)),
            dma((total,)),
            dma((total, 3)),
            dma((total, 3)),
            dma((total, 2)),
            dma((total,)),
            dma((total,)),
            dma((total, 3)),
            dma((total, 3)),
        ],
        compiler_params=pltpu.CompilerParams(
            collective_id=1, has_side_effects=True, vmem_limit_bytes=COMM_VMEM
        ),
        cost_estimate=pl.CostEstimate(flops=0, bytes_accessed=100_000_000, transcendentals=0),
    )(*grads)


def pack_rows(vectors):
    rows = [jnp.pad(v, (0, D - v.shape[0])) for v in vectors]
    rows += [jnp.zeros((D,), rows[0].dtype)] * (32 - len(rows))
    return jnp.stack(rows)[None]


def gather_shards(fast, shards):
    if fast:
        return gather_all(shards)
    return [lax.all_gather(s, "fsdp", axis=1, tiled=False) for s in shards]


def sum_shards(fast, grads):
    if fast:
        return sum_all([g.reshape(g.shape[0], 4, 2, g.shape[2], D) for g in grads])
    owned = [lax.psum_scatter(g, "fsdp", scatter_dimension=1, tiled=False) for g in grads]
    return [lax.psum(g, "dp") for g in owned]


def local(
    fast,
    hidden,
    image_feats,
    caption_counts,
    text_lengths,
    out_grad,
    self_query,
    query_bias,
    self_key,
    self_value,
    value_bias,
    self_output,
    output_bias,
    first_gain,
    first_shift,
    cross_query,
    crossquery_bias,
    cross_key,
    cross_value,
    crossvalue_bias,
    cross_output,
    crossoutput_bias,
    second_gain,
    second_shift,
    vision_gain,
    vision_shift,
    expand_weight,
    expand_bias,
    contract_weight,
    contract_bias,
    third_gain,
    third_shift,
):
    low = jnp.bfloat16
    vectors = (
        query_bias,
        value_bias,
        output_bias,
        first_gain,
        first_shift,
        crossquery_bias,
        crossvalue_bias,
        crossoutput_bias,
        second_gain,
        second_shift,
        contract_bias,
        third_gain,
        third_shift,
        vision_gain,
        vision_shift,
        expand_bias,
    )
    full = gather_shards(
        fast,
        (
            pack_rows(vectors),
            jnp.stack([self_query, self_key, self_value, self_output]),
            jnp.stack([cross_key, cross_value]),
            jnp.stack([cross_query, cross_output]),
            expand_weight.T[None],
            contract_weight[None],
        ),
    )
    rows = full[0].reshape(-1, 32, D)
    shards = rows.shape[0]
    (
        b_query,
        b_value,
        b_out,
        gain_one,
        shift_one,
        b_cquery,
        b_cvalue,
        b_cout,
        gain_two,
        shift_two,
        b_contract,
        gain_three,
        shift_three,
        gain_vision,
        shift_vision,
        b_expand,
    ) = (as_float(rows[:, i, : v.shape[0]].reshape(-1)) for i, v in enumerate(vectors))
    w_query, w_key, w_value, w_out = full[1].reshape(4, D, D)
    feat = image_feats.shape[-1]
    w_ckey, w_cvalue = full[2].reshape(2, feat, D)
    w_cquery, w_cout = full[3].reshape(2, D, D)
    w_expand_t = full[4].reshape(-1, D)
    w_contract = full[5].reshape(-1, D)

    scaling = HDIM ** (-0.5)
    captions = hidden.shape[0]
    images = image_feats.shape[0]
    bounds = jnp.cumsum(caption_counts[0], dtype=jnp.int32)
    positions = jnp.arange(captions, dtype=jnp.int32)
    image_index = jnp.sum(
        (positions[:, None] >= bounds[None, :]).astype(jnp.int32), axis=1, dtype=jnp.int32
    )
    row_image = jnp.repeat(image_index, NQ)
    key_image = jnp.repeat(jnp.arange(images, dtype=jnp.int32), PATCH)
    shown = row_image[:, None] == key_image[None, :]
    slots = jnp.arange(SEQ, dtype=jnp.int32)[None, :]
    key_valid = jnp.logical_or(slots < NQ, slots - NQ < text_lengths[:, None])
    query_low = (project(hidden, w_query) + b_query).astype(low)
    key_low = project(hidden, w_key).astype(low)
    value_low = (project(hidden, w_value) + b_value).astype(low)
    scores = (
        jnp.einsum(
            "cqhd,ckhd->chqk",
            heads_of(query_low),
            heads_of(key_low),
            preferred_element_type=jnp.float32,
        )
        * scaling
    )
    scores = jnp.where(key_valid[:, None, None, :], scores, MASKED)
    probs, soft_back = jax.vjp(softmax_rows, scores)
    probs_low = probs.astype(low)
    mixed_low = (
        jnp.einsum(
            "chqk,ckhd->cqhd", probs_low, heads_of(value_low), preferred_element_type=jnp.float32
        )
        .reshape(captions, SEQ, D)
        .astype(low)
    )
    branch = project(mixed_low, w_out) + b_out
    first, norm_back_one = jax.vjp(norm_rows, as_float(hidden) + branch, gain_one, shift_one)
    query_rows = first[:, :NQ]
    cross_in = query_rows.astype(low)
    cquery_low = (project(cross_in, w_cquery) + b_cquery).astype(low).reshape(-1, D)
    vision_vals, vision_back = jax.vjp(
        norm_rows, as_float(image_feats.reshape(-1, feat)), gain_vision, shift_vision
    )
    vision_low = vision_vals.astype(low)
    ckey_low = project(vision_low, w_ckey).astype(low)
    cvalue_low = (project(vision_low, w_cvalue) + b_cvalue).astype(low)
    cscores = (
        jnp.einsum(
            "qhd,khd->hqk",
            heads_of(cquery_low),
            heads_of(ckey_low),
            preferred_element_type=jnp.float32,
        )
        * scaling
    )
    cscores = jnp.where(shown[None], cscores, -jnp.inf)
    cprobs, csoft_back = jax.vjp(softmax_rows, cscores)
    cprobs_low = cprobs.astype(low)
    cmixed_low = (
        jnp.einsum(
            "hqk,khd->qhd", cprobs_low, heads_of(cvalue_low), preferred_element_type=jnp.float32
        )
        .reshape(captions, NQ, D)
        .astype(low)
    )
    cbranch = project(cmixed_low, w_cout) + b_cout
    second, norm_back_two = jax.vjp(norm_rows, query_rows + cbranch, gain_two, shift_two)
    joined = jnp.concatenate([second, first[:, NQ:]], axis=1)
    joined_low = joined.astype(low)
    widened = project_back(joined_low, w_expand_t) + b_expand
    active, gelu_back = jax.vjp(gelu_exact, widened)
    active_low = active.astype(low)
    narrowed = project(active_low, w_contract) + b_contract
    layer_out, norm_back_three = jax.vjp(norm_rows, joined + narrowed, gain_three, shift_three)

    grad_three_in, grad_gain_three, grad_shift_three = norm_back_three(as_float(out_grad))
    grad_narrow = grad_three_in.astype(low)
    grad_w_contract = weight_grad(active_low, grad_narrow)
    grad_b_contract = bias_grad(grad_narrow)
    (grad_wide,) = gelu_back(project_back(grad_narrow, w_contract))
    grad_wide_low = grad_wide.astype(low)
    grad_w_expand_t = weight_grad(grad_wide_low, joined_low)
    grad_b_expand = bias_grad(grad_wide_low)
    grad_joined = grad_three_in + project(grad_wide_low, w_expand_t)
    grad_two_in, grad_gain_two, grad_shift_two = norm_back_two(grad_joined[:, :NQ])
    grad_cbranch = grad_two_in.astype(low)
    grad_w_cout = weight_grad(cmixed_low, grad_cbranch)
    grad_b_cout = bias_grad(grad_cbranch)
    grad_cmixed = heads_of(project_back(grad_cbranch, w_cout).astype(low).reshape(-1, D))
    grad_cprobs = jnp.einsum(
        "qhd,khd->hqk", grad_cmixed, heads_of(cvalue_low), preferred_element_type=jnp.float32
    )
    grad_cvalue = (
        jnp.einsum("hqk,qhd->khd", cprobs_low, grad_cmixed, preferred_element_type=jnp.float32)
        .reshape(-1, D)
        .astype(low)
    )
    (grad_cscores,) = csoft_back(grad_cprobs)
    grad_cscores_low = grad_cscores.astype(low)
    grad_cquery = (
        (
            jnp.einsum(
                "hqk,khd->qhd",
                grad_cscores_low,
                heads_of(ckey_low),
                preferred_element_type=jnp.float32,
            )
            * scaling
        )
        .reshape(captions, NQ, D)
        .astype(low)
    )
    grad_ckey = (
        (
            jnp.einsum(
                "hqk,qhd->khd",
                grad_cscores_low,
                heads_of(cquery_low),
                preferred_element_type=jnp.float32,
            )
            * scaling
        )
        .reshape(-1, D)
        .astype(low)
    )
    grad_w_cquery = weight_grad(cross_in, grad_cquery)
    grad_b_cquery = bias_grad(grad_cquery)
    key_term = weight_grad(vision_low, grad_ckey)
    value_term = weight_grad(vision_low, grad_cvalue)
    value_bias_term = bias_grad(grad_cvalue)
    rows_grad = project_back(grad_ckey, w_ckey) + project_back(grad_cvalue, w_cvalue)
    unused_feats, grad_gain_vision, grad_shift_vision = vision_back(rows_grad)
    grad_first = jnp.concatenate(
        [grad_two_in + project_back(grad_cquery, w_cquery), grad_joined[:, NQ:]], axis=1
    )
    grad_one_in, grad_gain_one, grad_shift_one = norm_back_one(grad_first)
    grad_branch = grad_one_in.astype(low)
    grad_w_out = weight_grad(mixed_low, grad_branch)
    grad_b_out = bias_grad(grad_branch)
    grad_mixed = heads_of(project_back(grad_branch, w_out).astype(low))
    grad_probs = jnp.einsum(
        "cqhd,ckhd->chqk", grad_mixed, heads_of(value_low), preferred_element_type=jnp.float32
    )
    grad_value = (
        jnp.einsum("chqk,cqhd->ckhd", probs_low, grad_mixed, preferred_element_type=jnp.float32)
        .reshape(captions, SEQ, D)
        .astype(low)
    )
    (grad_scores,) = soft_back(grad_probs)
    grad_scores_low = grad_scores.astype(low)
    grad_query = (
        (
            jnp.einsum(
                "chqk,ckhd->cqhd",
                grad_scores_low,
                heads_of(key_low),
                preferred_element_type=jnp.float32,
            )
            * scaling
        )
        .reshape(captions, SEQ, D)
        .astype(low)
    )
    grad_key = (
        (
            jnp.einsum(
                "chqk,cqhd->ckhd",
                grad_scores_low,
                heads_of(query_low),
                preferred_element_type=jnp.float32,
            )
            * scaling
        )
        .reshape(captions, SEQ, D)
        .astype(low)
    )
    grad_w_query = weight_grad(hidden, grad_query)
    grad_b_query = bias_grad(grad_query)
    grad_w_key = weight_grad(hidden, grad_key)
    grad_w_value = weight_grad(hidden, grad_value)
    grad_b_value = bias_grad(grad_value)
    input_grad = (
        grad_one_in
        + project_back(grad_query, w_query)
        + project_back(grad_key, w_key)
        + project_back(grad_value, w_value)
    )
    vector_grads = (
        grad_b_query,
        grad_b_value,
        grad_b_out,
        grad_gain_one,
        grad_shift_one,
        grad_b_cquery,
        value_bias_term,
        grad_b_cout,
        grad_gain_two,
        grad_shift_two,
        grad_b_contract,
        grad_gain_three,
        grad_shift_three,
        grad_gain_vision,
        grad_shift_vision,
        grad_b_expand,
    )
    packed = jnp.stack(
        [
            jnp.pad(v.astype(low).reshape(shards, -1), ((0, 0), (0, D - v.shape[0] // shards)))
            for v in vector_grads
        ]
        + [jnp.zeros((shards, D), low)] * (32 - len(vector_grads)),
        axis=1,
    )

    def cut(*parts):
        return jnp.stack([p.astype(low).reshape(shards, -1, D) for p in parts])

    summed = sum_shards(
        fast,
        (
            packed[None],
            cut(grad_w_query, grad_w_key, grad_w_value, grad_w_out),
            cut(key_term, value_term),
            cut(grad_w_cquery, grad_w_cout),
            cut(grad_w_expand_t),
            cut(grad_w_contract),
        ),
    )
    sums = [as_float(s) for s in summed]
    vec = [sums[0][0, i, : v.shape[0]] for i, v in enumerate(vectors)]
    return (
        layer_out,
        input_grad,
        sums[1][0],
        vec[0],
        sums[1][1],
        sums[1][2],
        vec[1],
        sums[1][3],
        vec[2],
        vec[3],
        vec[4],
        sums[3][0],
        vec[5],
        sums[2][0],
        sums[2][1],
        vec[6],
        sums[3][1],
        vec[7],
        vec[8],
        vec[9],
        vec[13],
        vec[14],
        sums[4][0].T,
        vec[15],
        sums[5][0],
        vec[10],
        vec[11],
        vec[12],
    )


def solution(mesh):
    placed = (
        P(("dp", "fsdp"), None, None),
        P(("dp", "fsdp"), None, None),
        P(("dp", "fsdp"), None),
        P(("dp", "fsdp")),
        P(("dp", "fsdp"), None, None),
        P("fsdp", None),
        P("fsdp"),
        P("fsdp", None),
        P("fsdp", None),
        P("fsdp"),
        P("fsdp", None),
        P("fsdp"),
        P("fsdp"),
        P("fsdp"),
        P("fsdp", None),
        P("fsdp"),
        P("fsdp", None),
        P("fsdp", None),
        P("fsdp"),
        P("fsdp", None),
        P("fsdp"),
        P("fsdp"),
        P("fsdp"),
        P("fsdp"),
        P("fsdp"),
        P(None, "fsdp"),
        P("fsdp"),
        P("fsdp", None),
        P("fsdp"),
        P("fsdp"),
        P("fsdp"),
    )
    fast = mesh.shape["dp"] == 4 and mesh.shape["fsdp"] == 8
    return jax.shard_map(
        functools.partial(local, fast),
        mesh=mesh,
        in_specs=placed,
        out_specs=(
            P(("dp", "fsdp"), None, None),
            P(("dp", "fsdp"), None, None),
            P("fsdp", None),
            P("fsdp"),
            P("fsdp", None),
            P("fsdp", None),
            P("fsdp"),
            P("fsdp", None),
            P("fsdp"),
            P("fsdp"),
            P("fsdp"),
            P("fsdp", None),
            P("fsdp"),
            P("fsdp", None),
            P("fsdp", None),
            P("fsdp"),
            P("fsdp", None),
            P("fsdp"),
            P("fsdp"),
            P("fsdp"),
            P("fsdp"),
            P("fsdp"),
            P(None, "fsdp"),
            P("fsdp"),
            P("fsdp", None),
            P("fsdp"),
            P("fsdp"),
            P("fsdp"),
        ),
        check_vma=False,
    )
```

time: 1440 us -> 587 us (0.41)
  waiting for transfers between devices: 931 us -> 0 us
  Pallas kernels: 0 us -> 274 us
  blocking collectives: 107 us -> 0 us
  matrix products: 199 us -> 127 us
  between operations: 19.9 us -> 2.78 us
    reduce_scatter x6 -> x0, waiting for transfers between devices: 438 us -> none  [the longest x1 97.7 us: local(): lax.psum_scatter(grad_w_contract.astype(jnp.bfloat16), 'fsdp', scatter_di...]
    all_gather x10 -> x0, waiting for transfers between devices: 313 us -> none  [the longest x1 77.8 us: local(): lax.all_gather(expand_weight, 'fsdp', axis=1, tiled=True)]
    pallas_call x0 -> x2, Pallas kernels: none -> 274 us  [the longest x1 139 us: gather_all(): pl.pallas_call(gather_kernel, out_shape=[jax.ShapeDtypeStruct((count, 4,...]
    unnamed x25 -> x0, waiting for transfers between devices: 117 us -> none
    unnamed x2 -> x0, blocking collectives: 74.3 us -> none
    psum x1 -> x0, waiting for transfers between devices: 62.7 us -> none  [local(): lax.psum(owned[0].astype(jnp.bfloat16), 'dp').astype(jnp.float32)]
    dot_general x10, matrix products: 50.6 us -> 19.7 us  [weight_grad(): lax.dot_general(flat_operand, flat_upstream, (((0,), (0,)), ((), ())), pr...]
    unnamed x301 -> x230, local copies, waits for them, and re-layouts: 47 us -> 18.8 us
  transfers between devices with their start and end apart: 21 -> 0, of which waited for: 17 -> 0; matrix products, arithmetic and copies ran while one was open for 19% -> 0% of each run, Pallas kernels for 0% -> 0%
where the time goes in v1:
time: 587 us; the launch traced here: 579 us
  Pallas kernels  274 us (47%)
  matrix products  127 us (22%)
  local copies, waits for them, and re-layouts  106 us (18%)
  other arithmetic  68.5 us (12%)
    pallas_call x1, Pallas kernels, gather_all(): pl.pallas_call(gather_kernel, out_shape=[jax.ShapeDtypeStruct((count, 4,...  139 us
    pallas_call x1, Pallas kernels, sum_all(): pl.pallas_call(sum_kernel, out_shape=[jax.ShapeDtypeStruct((count, rows,...  135 us
    dot_general x10, matrix products, project_back(): jnp.einsum('...n,kn->...k', upstream, weight, preferred_element_type=jnp....  37.8 us
    dot_general x10, matrix products, project(): jnp.einsum('...k,kn->...n', operand, weight, preferred_element_type=jnp.f...  30.5 us
    dot_general x10, matrix products, weight_grad(): lax.dot_general(flat_operand, flat_upstream, (((0,), (0,)), ((), ())), pr...  19.7 us
    unnamed x230, local copies, waits for them, and re-layouts  18.8 us
    convert_element_type x1, other arithmetic, local(): active_low = active.astype(low)  15.3 us

profile of v1, /device:TPU:0, one launch (start us, length us, event | category | flops | bytes accessed | tf_op | source)
XLA Modules:
  0.0 579.3 jit_solution(6504518431502097392)
XLA Ops:
  19.1 139.5 %shard_map.510 = (bf16[1,4,2,32,768]{4,3,2,1,0:T(8,128)(2,1)}, bf16[4,4,2,96,768]{4,3,2,1,0:T(8,128)(2,1)}, bf16[2,4,2,176,768]{4,3,2,1,0:T(8,128)(2,1)}, bf16[2...) custom-call(bf16[1,32,768]{2,1,0:T(8,128)(2,1)} %bitcast.270, ...), custom_call_target="tpu_custom_call" | custom-call | bytes 100000000 | tf_op jit(solution)/shard_map/pallas_call | solution.py:219
  162.8 5.0 fusion.75
  169.5 2.8 fusion.20
  172.3 3.8 reshape.730
  178.2 2.8 fusion.21
  182.8 2.5 fusion.22
  187.7 2.4 fusion.10
  204.9 3.6 convert_element_type.545
  208.4 4.6 fusion.76
  213.1 5.3 add_convert_fusion.4
  218.4 2.9 copy.136
  225.4 5.4 convolution_convert_fusion.5
  230.8 2.5 copy.137
  233.3 3.0 fusion.1
  240.0 4.9 convert_reduce_fusion
  253.3 6.9 %fusion.16 = (u8[64,3072]{1,0:T(8,128)(4,1)S(1)}, u8[64,3072]{1,0:T(8,128)(4,1)S(1)}, f32[8,64,3072]{2,1,0:T(8,128)S(1)}) fusion(f32[3072]{0:T(1024)S(1)} %bitcast.277, bf16[3072,768,1]{1,0,2:T(8,128)(2,1)} %bitcast.285, f32[8,32,768]{2,1,0:T(8,128)S(1)} %copy-done.58, f32[8,32,768]{2,1,0:T(8,128)S(1)} %multiply_add_fusion.2), kind=kOutput, calls=%fused_computation.87 | convolution fusion | flops 2439118848 | bytes 12988416 | tf_op jit(solution)/shard_map/...n,kn->...k/dot_general | solution.py:41
  260.2 15.3 %multiply_convert_fusion = (bf16[8,64,3072]{2,1,0:T(8,128)(2,1)S(1)}, f32[8,64,3072]{2,1,0:T(8,128)}) fusion(f32[8,64,3072]{2,1,0:T(8,128)S(1)} %get-tuple-element.233, f32[3072]{0:T(1024)S(1)} %bitcast.278, u8[64,3072]{1,0:T(8,128)(4,1)S(1)} %get-tuple-element.137, u8[64,3072]{1,0:T(8,128)(4,1)S(1)} %get-tuple-element.136), kind=kLoop, calls=%fused_computation.19 | loop fusion | flops 111673344 | bytes 16134144 | tf_op jit(solution)/shard_map/convert_element_type | solution.py:581
  275.6 3.8 fusion.81
  281.7 4.4 fusion.14
  286.8 2.8 fusion.65
  289.6 9.8 %fusion.86 = (bf16[3072]{0:T(1024)(128)(2,1)}, bf16[8,64,3072]{2,1,0:T(8,128)(2,1)S(1)}) fusion(f32[8,64,3072]{2,1,0:T(8,128)} %get-tuple-element.186, bf16[8,64,768]{2,1,0:T(8,128)(2,1)S(1)} %get-tuple-element.168, bf16[3072,768,1]{1,0,2:T(8,128)(2,1)} %bitcast.289, f32[8,64,3072]{2,1,0:T(8,128)} %copy-done.24, f32[3072]{0:T(1024)S(1)} %bitcast.279), kind=kOutput, calls=%fused_computation.242 | convolution fusion | flops 2441081856 | bytes 21252096 | tf_op jit(solution)/shard_map/...n,kn->...k/dot_general | solution.py:41
  299.4 2.7 add_add_fusion.5
  310.8 6.7 %multiply_reduce_fusion = (f32[12,256]{1,0:T(8,128)S(1)}, f32[12,256,771]{1,2,0:T(8,128)S(1)}) fusion(f32[12,256]{1,0:T(8,128)S(1)} %multiply_divide_fusion.1, f32[12,256]{1,0:T(8,128)S(1)} %get-tuple-element.229, f32[12,256,771]{1,2,0:T(8,128)} %copy-done, pred[256,771]{0,1:T(8,128)(4,1)S(1)} %broadcast_compare_fusion, bf16[256,12,64]{0,2,1:T(8,128)(2,1)S(1)} %copy.140, ...), kind=kOutput, calls=%fused_computation.3 | convolution fusion | flops 317377536 | bytes 20759808 | tf_op jit(solution)/shard_map/qhd,khd->hqk/dot_general | solution.py:599
  317.6 3.2 fusion.71
  320.8 3.1 fusion.85
  326.3 3.0 convert_element_type.584
  329.3 2.5 fusion.84
  336.8 3.8 reshape.739
  340.6 5.1 convert_reduce_fusion.2
  348.5 2.5 copy.150
  351.1 4.0 convert_element_type.594
  355.1 3.6 fusion.88
  363.2 3.3 fusion.87
  366.4 2.9 fusion.83
  369.4 2.4 copy.152
  371.8 4.1 convert_element_type.597
  375.9 4.1 add_add_fusion.2
  380.9 5.2 bitcast_reduce_fusion
  386.9 2.6 reshape.764
  389.6 6.3 %multiply_convert_fusion.3 = bf16[12,64,771]{2,1,0:T(8,128)(2,1)S(1)} fusion(bf16[256,12,64]{0,2,1:T(8,128)(2,1)S(1)} %copy-done.31, f32[12,256,771]{1,2,0:T(8,128)} %copy-done.2, pred[12,256,771]{1,2,0:T(8,128)(4,1)} %get-tuple-element.182, f32[12,256]{1,0:T(8,128)S(1)} %negate_divide_fusion.1), kind=kOutput, calls=%fused_computation.50 | convolution fusion | flops 311459328 | bytes 13432320 | tf_op jit(solution)/shard_map/hqk,qhd->khd/dot_general | solution.py:624
  399.7 3.1 fusion.64
  403.2 2.8 stack.212.refs_0_
  411.0 2.4 pad_maximum_fusion.refs_1_
  413.5 2.5 convolution_convert_fusion
  416.0 2.5 convolution_convert_fusion.1
  426.1 4.4 bitcast_convert_fusion.1
  430.5 4.7 bitcast_convert_fusion
  435.2 135.0 %shard_map.511 = (bf16[1,32,768]{2,1,0:T(8,128)(2,1)}, bf16[4,96,768]{2,1,0:T(8,128)(2,1)}, bf16[2,176,768]{2,1,0:T(8,128)(2,1)}, bf16[2,96,768]{2,1,0:T(8,128)(...) custom-call(bf16[1,4,2,32,768]{4,3,2,1,0:T(8,128)(2,1)} %stack.212.refs_0_, ...), custom_call_target="tpu_custom_call" | custom-call | bytes 100000000 | tf_op jit(solution)/shard_map/pallas_call | solution.py:368
  (429 shorter events, 114.0 us)
Async XLA Ops:
  0.7 16.6 %copy-start.76 = (bf16[96,768]{1,0:T(8,128)(2,1)S(1)}, bf16[96,768]{1,0:T(8,128)(2,1)}, u32[]{:S(2)}) copy-start(bf16[96,768]{1,0:T(8,128)(2,1)} %param.50) | copy-start | bytes 442372
  0.7 16.6 %copy-start.77 = (bf16[96,768]{1,0:T(8,128)(2,1)S(1)}, bf16[96,768]{1,0:T(8,128)(2,1)}, u32[]{:S(2)}) copy-start(bf16[96,768]{1,0:T(8,128)(2,1)} %param.45) | copy-start | bytes 442372
  0.7 17.4 %copy-start.73 = (bf16[768,384]{1,0:T(8,128)(2,1)S(1)}, bf16[768,384]{1,0:T(8,128)(2,1)}, u32[]{:S(2)}) copy-start(bf16[768,384]{1,0:T(8,128)(2,1)} %param.56) | copy-start | bytes 1769476
  167.8 10.4 %copy-start.53 = (bf16[1,4,2,96,768]{4,3,2,1,0:T(8,128)(2,1)}, bf16[1,4,2,96,768]{4,3,2,1,0:T(8,128)(2,1)S(1)}, u32[]{:S(2)}) copy-start(bf16[1,4,2,96,768]{4,3,2,1,0:T(8,128)(2,1)S(1)} %get-tuple-element.190) | copy-start | bytes 3538948
  167.8 15.0 %copy-start.55 = (bf16[1,4,2,96,768]{4,3,2,1,0:T(8,128)(2,1)}, bf16[1,4,2,96,768]{4,3,2,1,0:T(8,128)(2,1)S(1)}, u32[]{:S(2)}) copy-start(bf16[1,4,2,96,768]{4,3,2,1,0:T(8,128)(2,1)S(1)} %get-tuple-element.189) | copy-start | bytes 3538948
  182.8 4.9 copy-start.10
  193.0 93.1 %copy-start.69 = (f32[8,12,64]{2,1,0:T(8,128)}, f32[8,12,64]{2,1,0:T(8,128)S(1)}, u32[]{:S(2)}) copy-start(f32[8,12,64]{2,1,0:T(8,128)S(1)} %fusion.37) | copy-start | bytes 73732
  208.4 4.6 copy-start.89
  225.4 7.9 %copy-start.30 = (bf16[256,12,64]{0,2,1:T(8,128)(2,1)}, bf16[256,12,64]{0,2,1:T(8,128)(2,1)S(1)}, u32[]{:S(2)}) copy-start(bf16[256,12,64]{0,2,1:T(8,128)(2,1)S(1)} %copy.138) | copy-start | bytes 1179652
  240.0 7.1 %copy-start.15 = (bf16[771,768]{0,1:T(8,128)(2,1)S(1)}, bf16[771,768]{0,1:T(8,128)(2,1)}, u32[]{:S(2)}) copy-start(bf16[771,768]{0,1:T(8,128)(2,1)} %copy.136) | copy-start | bytes 3552772
  252.2 23.3 %slice-start.7 = ((s8[4718592]{0:T(1024)(128)(4,1)}), s8[4194304]{0:T(1024)(128)(4,1)S(1)}, s32[]{:S(2)}) async-start(s8[4718592]{0:T(1024)(128)(4,1)} %bitcast.290), calls=%async_computation.7 | async-start | bytes 8388608
  253.3 22.2 %copy-start.60 = (f32[8,32,768]{2,1,0:T(8,128)}, f32[8,32,768]{2,1,0:T(8,128)S(1)}, u32[]{:S(2)}) copy-start(f32[8,32,768]{2,1,0:T(8,128)S(1)} %multiply_add_fusion.2) | copy-start | bytes 2359300
  253.3 22.2 %slice-start.8 = ((s8[4718592]{0:T(1024)(128)(4,1)}), s8[524288]{0:T(1024)(128)(4,1)S(1)}, s32[]{:S(2)}) async-start(s8[4718592]{0:T(1024)(128)(4,1)} %bitcast.290), calls=%async_computation.8 | async-start | bytes 1048576
  260.2 15.3 %copy-start.24 = (f32[8,64,3072]{2,1,0:T(8,128)}, f32[8,64,3072]{2,1,0:T(8,128)S(1)}, u32[]{:S(2)}) copy-start(f32[8,64,3072]{2,1,0:T(8,128)S(1)} %get-tuple-element.233) | copy-start | bytes 18874372
  260.2 15.4 %copy-start.101 = (f32[768]{0:T(1024)S(1)}, f32[768]{0:T(1024)}, u32[]{:S(2)}) copy-start(f32[768]{0:T(1024)} %reshape.761) | copy-start | bytes 9220
  281.7 5.1 copy-start.9
  286.8 12.6 %slice-start.5 = ((s8[4718592]{0:T(1024)(128)(4,1)}), s8[4194304]{0:T(1024)(128)(4,1)S(1)}, s32[]{:S(2)}) async-start(s8[4718592]{0:T(1024)(128)(4,1)} %bitcast.286), calls=%async_computation.5 | async-start | bytes 8388608
  289.6 9.8 %copy-start.62 = (bf16[8,64,768]{2,1,0:T(8,128)(2,1)}, bf16[8,64,768]{2,1,0:T(8,128)(2,1)S(1)}, u32[]{:S(2)}) copy-start(bf16[8,64,768]{2,1,0:T(8,128)(2,1)S(1)} %get-tuple-element.168) | copy-start | bytes 2359300
  289.6 9.8 %copy-start.20 = (bf16[8,64,768]{2,1,0:T(8,128)(2,1)S(1)}, bf16[8,64,768]{2,1,0:T(8,128)(2,1)}, u32[]{:S(2)}) copy-start(bf16[8,64,768]{2,1,0:T(8,128)(2,1)} %param.35) | copy-start | bytes 2359300
  289.6 9.8 %slice-start.6 = ((s8[4718592]{0:T(1024)(128)(4,1)}), s8[524288]{0:T(1024)(128)(4,1)S(1)}, s32[]{:S(2)}) async-start(s8[4718592]{0:T(1024)(128)(4,1)} %bitcast.286), calls=%async_computation.6 | async-start | bytes 1048576
  308.8 8.7 %slice-start = ((s8[9535488]{0:T(1024)(128)(4,1)}), s8[1146880]{0:T(1024)(128)(4,1)S(1)}, s32[]{:S(2)}) async-start(s8[9535488]{0:T(1024)(128)(4,1)} %bitcast.224), calls=%async_computation | async-start | bytes 2293760
  310.7 6.8 %copy-start.32 = (bf16[256,12,64]{0,2,1:T(8,128)(2,1)}, bf16[256,12,64]{0,2,1:T(8,128)(2,1)S(1)}, u32[]{:S(2)}) copy-start(bf16[256,12,64]{0,2,1:T(8,128)(2,1)S(1)} %copy.140) | copy-start | bytes 1179652
  310.8 6.8 %slice-start.1 = ((s8[9535488]{0:T(1024)(128)(4,1)}), s8[4194304]{0:T(1024)(128)(4,1)S(1)}, s32[]{:S(2)}) async-start(s8[9535488]{0:T(1024)(128)(4,1)} %bitcast.224), calls=%async_computation.1 | async-start | bytes 8388608
  310.8 6.8 %slice-start.2 = ((s8[9535488]{0:T(1024)(128)(4,1)}), s8[4194304]{0:T(1024)(128)(4,1)S(1)}, s32[]{:S(2)}) async-start(s8[9535488]{0:T(1024)(128)(4,1)} %bitcast.224), calls=%async_computation.2 | async-start | bytes 8388608
  324.4 4.8 copy-start.22
  326.3 5.5 copy-start.23
  335.1 5.5 copy-start.6
  335.1 5.5 copy-start.68
  335.1 5.5 copy-start.78
  335.1 5.5 copy-start.92
  340.6 5.1 copy-start.7
  340.6 5.1 copy-start.70
  369.4 6.5 %copy-start.13 = (f32[8,64,768]{2,1,0:T(8,128)S(1)}, f32[8,64,768]{2,1,0:T(8,128)}, u32[]{:S(2)}) copy-start(f32[8,64,768]{2,1,0:T(8,128)} %copy-done.12) | copy-start | bytes 4718596
  369.4 6.5 %copy-start.27 = (bf16[1,4,2,96,768]{4,3,2,1,0:T(8,128)(2,1)S(1)}, bf16[1,4,2,96,768]{4,3,2,1,0:T(8,128)(2,1)}, u32[]{:S(2)}) copy-start(bf16[1,4,2,96,768]{4,3,2,1,0:T(8,128)(2,1)} %copy-done.26) | copy-start | bytes 3538948
  375.9 4.6 copy-start.83
  375.9 4.6 copy-start.84
  375.9 4.7 copy-start.100
  375.9 4.8 copy-start.33
  380.8 5.4 copy-start.98
  380.8 5.5 copy-start.97
  380.8 5.6 copy-start.96
  380.8 5.7 copy-start.95
  380.8 5.8 copy-start.93
  380.8 5.9 %copy-start.94 = (bf16[768]{0:T(1024)(128)(2,1)S(1)}, bf16[768]{0:T(1024)(128)(2,1)}, u32[]{:S(2)}) copy-start(bf16[768]{0:T(1024)(128)(2,1)} %get-tuple-element.205) | copy-start | bytes 4612
  380.8 6.1 %copy-start.4 = (bf16[3,257,1408]{2,1,0:T(8,128)(2,1)S(1)}, bf16[3,257,1408]{2,1,0:T(8,128)(2,1)}, u32[]{:S(2)}) copy-start(bf16[3,257,1408]{2,1,0:T(8,128)(2,1)} %param.32) | copy-start | bytes 6513412
  389.6 6.4 %copy-start.41 = (bf16[1,4,2,176,768]{4,3,2,1,0:T(8,128)(2,1)S(1)}, bf16[1,4,2,176,768]{4,3,2,1,0:T(8,128)(2,1)}, u32[]{:S(2)}) copy-start(bf16[1,4,2,176,768]{4,3,2,1,0:T(8,128)(2,1)} %get-tuple-element.192) | copy-start | bytes 6488068
  389.6 8.7 %slice-start.3 = ((s8[4370432]{0:T(1024)(128)(4,1)}), s8[176128]{0:T(1024)(128)(4,1)S(1)}, s32[]{:S(2)}) async-start(s8[4370432]{0:T(1024)(128)(4,1)} %bitcast.242), calls=%async_computation.3 | async-start | bytes 352256
  399.7 6.3 %copy-start.47 = (bf16[8,12,64,64]{3,2,1,0:T(8,128)(2,1)S(1)}, bf16[8,12,64,64]{3,2,1,0:T(8,128)(2,1)}, u32[]{:S(2)}) copy-start(bf16[8,12,64,64]{3,2,1,0:T(8,128)(2,1)} %copy-done.46) | copy-start | bytes 2359300
  (66 other events, 171.4 us)
